TPU v7x, 512 devices: a whole 4x8x8 slice. The times are simulated.
512 devices in a mesh: tm: 32 (over y, x), dom: 16 (over z, core).
Axes of the slice: x: 4, y: 8, z: 8, core: 2. Of those that a mesh axis runs over, the one named last changes fastest.
Arguments:
- node_pos: float32 [32, 3, 3, 8192], P('tm', None, None, 'dom'), may hold values from -2 to 19
- vorticity: float32 [3, 8192], P(None, 'dom'), may hold values from -0.024414062 to 0.024414062
- coarse_of: int32 [8192], P('dom'), may hold values from 0 to 4095, as said below
Outputs:
- fine_nodes: float32 [32, 3, 3, 8192], P('tm', None, None, 'dom')
- coarse_end: float32 [32, 3, 4096], P('tm', None, 'dom')
Inputs may be any that keep to these rules, and one draw needn't show every extreme that they name: coarse_of[i] = (i // 2 + j) mod 4096 for some integer j with -2048 <= j <= 2048; j = 0 for even i; j = 2048 for i = 1 and j = -2048 for i = 3.
All inputs are finite; a program needn't handle non-finite values.
Results may differ from a plain program's by a relative error of at most 0.0003.
Values sent between devices are 32-bit elements; how exact they have to be, the bound alone decides.
No kernel may reach another device: no remote copies, remote signals or barrier semaphores. Data moves between devices by JAX's collectives and lax.ppermute only.
A program may use at most 64 MiB of HBM per device.

v0:
```python
import math

import jax
import jax.numpy as jnp
from jax import lax
from jax.sharding import PartitionSpec as P

inv_four_pi = 1.0 / (4.0 * math.pi)
sigma_sq = 0.01
dt_slice = 0.5
node_weights = ((5.0 / 24.0, 1.0 / 3.0, -1.0 / 24.0), (-1.0 / 24.0, 1.0 / 3.0, 5.0 / 24.0))


def passed_along(block, axis, distance):
    devices = range(lax.axis_size(axis))
    route = [(i - distance, i) for i in devices if i - distance in devices]
    return lax.ppermute(block, axis, route)


def pair_field(targets, sources, strengths):
    offsets = targets[:, :, None] - sources[:, None, :]
    radius_sq = jnp.sum(offsets * offsets, axis=0) + sigma_sq
    kernel = inv_four_pi / (radius_sq * jnp.sqrt(radius_sq))
    moments = jnp.concatenate([strengths, jnp.cross(strengths, sources, axis=0)], 0)
    summed = jnp.einsum("ts,cs->ct", kernel, moments, precision=lax.Precision.HIGHEST)
    return jnp.cross(summed[:3], targets, axis=0) - summed[3:]


def accumulate_field(targets, count_nodes, running, source_block):
    width_total = source_block.shape[2]
    block_width = math.gcd(width_total, 1024)

    def one_block(block_number, partial_value):
        offset = block_number * block_width
        chosen = lax.dynamic_slice_in_dim(source_block, offset, block_width, 2)
        added = [
            pair_field(targets[node_index], chosen[node_index], chosen[count_nodes])
            for node_index in range(count_nodes)
        ]
        return partial_value + jnp.stack(added, 0)

    return lax.fori_loop(0, width_total // block_width, one_block, running)


def swept_field(positions, vorticity):
    stacked = jnp.stack([positions, vorticity], 0)
    empty = jnp.zeros((1,) + positions.shape, jnp.float32)
    result = accumulate_field(
        positions[None], 1, empty, lax.all_gather(stacked, "dom", axis=2, tiled=True)
    )
    return result[0]


def body(node_pos, vorticity, coarse_of):
    states = node_pos[0]
    particles = vorticity.shape[1]
    domains = lax.axis_size("dom")
    coarse_dev = particles // 2
    coarse_all = coarse_dev * domains
    stacked = jnp.concatenate([states, vorticity[None]], 0)
    velocity = accumulate_field(
        states,
        3,
        jnp.zeros(states.shape, jnp.float32),
        lax.all_gather(stacked, "dom", axis=2, tiled=True),
    )
    quad_old = [
        dt_slice * (row[0] * velocity[0] + row[1] * velocity[1] + row[2] * velocity[2])
        for row in node_weights
    ]
    first = states[0]
    second = first + quad_old[0]
    swept_two = swept_field(second, vorticity)
    third = second + 0.5 * dt_slice * (swept_two - velocity[1]) + quad_old[1]
    swept_three = swept_field(third, vorticity)
    quad_new = [
        dt_slice * (row[0] * velocity[0] + row[1] * swept_two + row[2] * swept_three)
        for row in node_weights
    ]
    ones_row = jnp.ones((1, particles), jnp.float32)
    rows_all = jnp.concatenate([first, second, third, quad_new[0], quad_new[1], ones_row], 0)
    selector = (coarse_of[:, None] == lax.iota(jnp.int32, coarse_all)[None, :]).astype(jnp.float32)
    partial_value = jnp.dot(rows_all, selector, precision=lax.Precision.HIGHEST)
    owned = lax.psum_scatter(partial_value, "dom", scatter_dimension=1, tiled=True)
    means = owned[:15] / owned[15:16]
    built = means[:9].reshape(3, 3, coarse_dev)
    early = means[9:12]
    late = means[12:15]
    advance = early + late
    slice_index = lax.axis_index("tm")
    slices = lax.axis_size("tm")

    def relay(turn_index, current):
        received = passed_along(current + advance, "tm", 1)
        return jnp.where(slice_index == 0, built[0], received)

    begin = lax.fori_loop(0, slices - 1, relay, built[0])
    ends = jnp.stack([begin, begin + early, begin + advance], 0)
    correction = (ends - built).reshape(9, coarse_dev)
    window = lax.all_gather(correction, "dom", axis=1, tiled=True)
    spread = jnp.einsum("cq,pq->cp", window, selector, precision=lax.Precision.HIGHEST)
    fine_nodes = jnp.stack([first, second, third], 0) + spread.reshape(3, 3, particles)
    return (fine_nodes[None], (begin + advance)[None])


def solution(mesh):
    return jax.shard_map(
        body,
        mesh=mesh,
        in_specs=(P("tm", None, None, "dom"), P(None, "dom"), P("dom")),
        out_specs=(P("tm", None, None, "dom"), P("tm", None, "dom")),
        check_vma=False,
    )
```

profile of v0, /device:TPU:33, one launch (start us, length us, event | category | flops | bytes accessed | tf_op | source)
XLA Modules:
  0.0 572.6 jit_solution(7613166318234151924)
XLA Ops:
  9.3 25.1 %all_gather.12 = f32[4,3,8192]{2,1,0:T(4,128)S(1)} all-gather(f32[4,3,512]{2,1,0:T(4,128)S(1)} %pad_maximum_fusion.6), channel_id=1, replica_groups=mesh['tm'=32,'dom'=16] {'dom'}, dimensions={2}, use_global_device_ids=true | all-gather | bytes 417792 | tf_op jit(solution)/shard_map/all_gather | solution.py:65
  34.4 87.2 %while.55 = (s32[]{:T(128)}, f32[3,3,512]{2,1,0:T(4,128)S(1)}, f32[4,3,8192]{2,1,0:T(4,128)S(1)}, f32[3,3,512]{2,1,0:T(4,128)S(1)}, s32[]{:T(128)}, /*index=5*/s...) while((s32[]{:T(128)}, f32[3,3,512]{2,1,0:T(4,128)S(1)}, ...), condition=%wide.region_4.0_spmd.clone, body=%wide.region_0.0_spmd.clone.sunk | while | flops 130676744 | bytes 13265113 | solution.py:42
  121.7 15.4 %all_gather.13 = f32[2,3,8192]{2,1,0:T(4,128)S(1)} all-gather(f32[2,3,512]{2,1,0:T(4,128)S(1)} %pad_maximum_fusion.8), channel_id=1, replica_groups=mesh['tm'=32,'dom'=16] {'dom'}, dimensions={2}, use_global_device_ids=true | all-gather | bytes 208896 | tf_op jit(solution)/shard_map/all_gather | solution.py:49
  137.0 28.0 %while.56 = (s32[]{:T(128)}, f32[1,3,512]{2,1,0:T(4,128)S(1)}, f32[2,3,8192]{2,1,0:T(4,128)S(1)}, f32[3,512]{1,0:T(4,128)S(1)}, s32[]{:T(128)}, /*index=5*/s32[]{:T(128)}, s32[]{}, s32[]{:T(128)}, s32[]{:T(128)}) while((s32[]{:T(128)}, f32[1,3,512]{2,1,0:T(4,128)S(1)}, f32[2,3,8192]{2,1,0:T(4,128)S(1)}, f32[3,512]{1,0:T(4,128)S(1)}, ...), condition=%wide.region_7.0_spmd.clone, body=%wide.region_5.0_spmd.clone.sunk | while | flops 43555848 | bytes 4415657 | solution.py:42
  165.1 16.5 %all_gather.14 = f32[2,3,8192]{2,1,0:T(4,128)S(1)} all-gather(f32[2,3,512]{2,1,0:T(4,128)S(1)} %pad_maximum_fusion.7), channel_id=1, replica_groups=mesh['tm'=32,'dom'=16] {'dom'}, dimensions={2}, use_global_device_ids=true | all-gather | bytes 208896 | tf_op jit(solution)/shard_map/all_gather | solution.py:49
  181.6 28.0 %while.57 = (s32[]{:T(128)}, f32[1,3,512]{2,1,0:T(4,128)S(1)}, f32[2,3,8192]{2,1,0:T(4,128)S(1)}, f32[3,512]{1,0:T(4,128)S(1)}, s32[]{:T(128)}, /*index=5*/s32[]{:T(128)}, s32[]{}, s32[]{:T(128)}, s32[]{:T(128)}) while((s32[]{:T(128)}, f32[1,3,512]{2,1,0:T(4,128)S(1)}, f32[2,3,8192]{2,1,0:T(4,128)S(1)}, f32[3,512]{1,0:T(4,128)S(1)}, ...), condition=%wide.region_10.0_spmd.clone, body=%wide.region_8.0_spmd.clone.sunk | while | flops 43555848 | bytes 4415657 | solution.py:42
  213.3 53.9 %reduce-scatter.2.cloned.1.call-done = f32[16,256]{1,0:T(8,128)} async-done(((f32[16,4096]{1,0:T(8,128)}), f32[16,256]{1,0:T(8,128)}) %reduce-scatter.2.cloned.1.call-update) | async-done | bytes 16400 | tf_op jit(solution)/shard_map/reduce_scatter | solution.py:84
  268.6 237.9 %while.54 = (s32[]{:T(128)}, f32[3,256]{1,0:T(4,128)S(1)}, pred[]{:T(512)}, f32[3,3,256]{2,1,0:T(4,128)S(1)}, f32[3,256]{1,0:T(4,128)S(1)}, /*index=5*/s32[]{:T(128)}) while((s32[]{:T(128)}, f32[3,256]{1,0:T(4,128)S(1)}, pred[]{:T(512)}, f32[3,3,256]{2,1,0:T(4,128)S(1)}, f32[3,256]{1,0:T(4,128)S(1)}, /*index=5*/s32[]{:T(128)}) %tuple.200), condition=%wide.region_13.16_spmd, body=%wide.region_12.15_spmd.sunk | while | flops 1538 | bytes 30830 | solution.py:97
  278.2 5.7 %collective-permute-done = f32[3,256]{1,0:T(4,128)S(1)} collective-permute-done((f32[3,256]{1,0:T(4,128)S(1)}, f32[3,256]{1,0:T(4,128)S(1)}, u32[]{:S(2)}, u32[]{:S(2)}) %collective-permute-start) | collective-permute-done | bytes 3104 | tf_op jit(solution)/shard_map/while/body/eval_jaxpr/ppermute | solution.py:17
  285.9 5.7 %collective-permute-done = f32[3,256]{1,0:T(4,128)S(1)} collective-permute-done((f32[3,256]{1,0:T(4,128)S(1)}, f32[3,256]{1,0:T(4,128)S(1)}, u32[]{:S(2)}, u32[]{:S(2)}) %collective-permute-start) | collective-permute-done | bytes 3104 | tf_op jit(solution)/shard_map/while/body/eval_jaxpr/ppermute | solution.py:17
  293.6 5.7 %collective-permute-done = f32[3,256]{1,0:T(4,128)S(1)} collective-permute-done((f32[3,256]{1,0:T(4,128)S(1)}, f32[3,256]{1,0:T(4,128)S(1)}, u32[]{:S(2)}, u32[]{:S(2)}) %collective-permute-start) | collective-permute-done | bytes 3104 | tf_op jit(solution)/shard_map/while/body/eval_jaxpr/ppermute | solution.py:17
  301.3 5.8 %collective-permute-done = f32[3,256]{1,0:T(4,128)S(1)} collective-permute-done((f32[3,256]{1,0:T(4,128)S(1)}, f32[3,256]{1,0:T(4,128)S(1)}, u32[]{:S(2)}, u32[]{:S(2)}) %collective-permute-start) | collective-permute-done | bytes 3104 | tf_op jit(solution)/shard_map/while/body/eval_jaxpr/ppermute | solution.py:17
  309.0 5.7 %collective-permute-done = f32[3,256]{1,0:T(4,128)S(1)} collective-permute-done((f32[3,256]{1,0:T(4,128)S(1)}, f32[3,256]{1,0:T(4,128)S(1)}, u32[]{:S(2)}, u32[]{:S(2)}) %collective-permute-start) | collective-permute-done | bytes 3104 | tf_op jit(solution)/shard_map/while/body/eval_jaxpr/ppermute | solution.py:17
  324.3 5.7 %collective-permute-done = f32[3,256]{1,0:T(4,128)S(1)} collective-permute-done((f32[3,256]{1,0:T(4,128)S(1)}, f32[3,256]{1,0:T(4,128)S(1)}, u32[]{:S(2)}, u32[]{:S(2)}) %collective-permute-start) | collective-permute-done | bytes 3104 | tf_op jit(solution)/shard_map/while/body/eval_jaxpr/ppermute | solution.py:17
  332.0 5.7 %collective-permute-done = f32[3,256]{1,0:T(4,128)S(1)} collective-permute-done((f32[3,256]{1,0:T(4,128)S(1)}, f32[3,256]{1,0:T(4,128)S(1)}, u32[]{:S(2)}, u32[]{:S(2)}) %collective-permute-start) | collective-permute-done | bytes 3104 | tf_op jit(solution)/shard_map/while/body/eval_jaxpr/ppermute | solution.py:17
  339.7 5.7 %collective-permute-done = f32[3,256]{1,0:T(4,128)S(1)} collective-permute-done((f32[3,256]{1,0:T(4,128)S(1)}, f32[3,256]{1,0:T(4,128)S(1)}, u32[]{:S(2)}, u32[]{:S(2)}) %collective-permute-start) | collective-permute-done | bytes 3104 | tf_op jit(solution)/shard_map/while/body/eval_jaxpr/ppermute | solution.py:17
  347.3 5.7 %collective-permute-done = f32[3,256]{1,0:T(4,128)S(1)} collective-permute-done((f32[3,256]{1,0:T(4,128)S(1)}, f32[3,256]{1,0:T(4,128)S(1)}, u32[]{:S(2)}, u32[]{:S(2)}) %collective-permute-start) | collective-permute-done | bytes 3104 | tf_op jit(solution)/shard_map/while/body/eval_jaxpr/ppermute | solution.py:17
  355.0 5.7 %collective-permute-done = f32[3,256]{1,0:T(4,128)S(1)} collective-permute-done((f32[3,256]{1,0:T(4,128)S(1)}, f32[3,256]{1,0:T(4,128)S(1)}, u32[]{:S(2)}, u32[]{:S(2)}) %collective-permute-start) | collective-permute-done | bytes 3104 | tf_op jit(solution)/shard_map/while/body/eval_jaxpr/ppermute | solution.py:17
  362.7 5.7 %collective-permute-done = f32[3,256]{1,0:T(4,128)S(1)} collective-permute-done((f32[3,256]{1,0:T(4,128)S(1)}, f32[3,256]{1,0:T(4,128)S(1)}, u32[]{:S(2)}, u32[]{:S(2)}) %collective-permute-start) | collective-permute-done | bytes 3104 | tf_op jit(solution)/shard_map/while/body/eval_jaxpr/ppermute | solution.py:17
  370.3 5.7 %collective-permute-done = f32[3,256]{1,0:T(4,128)S(1)} collective-permute-done((f32[3,256]{1,0:T(4,128)S(1)}, f32[3,256]{1,0:T(4,128)S(1)}, u32[]{:S(2)}, u32[]{:S(2)}) %collective-permute-start) | collective-permute-done | bytes 3104 | tf_op jit(solution)/shard_map/while/body/eval_jaxpr/ppermute | solution.py:17
  378.0 5.7 %collective-permute-done = f32[3,256]{1,0:T(4,128)S(1)} collective-permute-done((f32[3,256]{1,0:T(4,128)S(1)}, f32[3,256]{1,0:T(4,128)S(1)}, u32[]{:S(2)}, u32[]{:S(2)}) %collective-permute-start) | collective-permute-done | bytes 3104 | tf_op jit(solution)/shard_map/while/body/eval_jaxpr/ppermute | solution.py:17
  385.7 5.7 %collective-permute-done = f32[3,256]{1,0:T(4,128)S(1)} collective-permute-done((f32[3,256]{1,0:T(4,128)S(1)}, f32[3,256]{1,0:T(4,128)S(1)}, u32[]{:S(2)}, u32[]{:S(2)}) %collective-permute-start) | collective-permute-done | bytes 3104 | tf_op jit(solution)/shard_map/while/body/eval_jaxpr/ppermute | solution.py:17
  393.4 5.7 %collective-permute-done = f32[3,256]{1,0:T(4,128)S(1)} collective-permute-done((f32[3,256]{1,0:T(4,128)S(1)}, f32[3,256]{1,0:T(4,128)S(1)}, u32[]{:S(2)}, u32[]{:S(2)}) %collective-permute-start) | collective-permute-done | bytes 3104 | tf_op jit(solution)/shard_map/while/body/eval_jaxpr/ppermute | solution.py:17
  507.1 54.0 %all_gather.15 = f32[9,4096]{1,0:T(8,128)S(1)} all-gather(f32[9,256]{1,0:T(8,128)S(1)} %slice_subtract_fusion.5), channel_id=1, replica_groups=mesh['tm'=32,'dom'=16] {'dom'}, dimensions={1}, use_global_device_ids=true | all-gather | bytes 156672 | tf_op jit(solution)/shard_map/all_gather | solution.py:100
  (417 shorter events, 305.1 us)
Async XLA Ops:
  7.2 260.0 %reduce-scatter.2.cloned.1.call-start = ((), (), s32[]{:S(2)}) async-start(), calls=%async_computation.1 | async-start | bytes 278528 | tf_op jit(solution)/shard_map/reduce_scatter | solution.py:84
  268.6 7.7 %collective-permute-start = (f32[3,256]{1,0:T(4,128)S(1)}, f32[3,256]{1,0:T(4,128)S(1)}, u32[]{:S(2)}, u32[]{:S(2)}) collective-permute-start(f32[3,256]{1,0:T(4,128)S(1)} %add.322), channel_id=1, source_target_pairs={{0,16},{16,32},{32,48},{48,64},{64,80},{80,96},{96,112},{112,128},... | collective-permute-start | bytes 9224 | tf_op jit(solution)/shard_map/while/body/eval_jaxpr/ppermute | solution.py:17
  276.3 7.7 %collective-permute-start = (f32[3,256]{1,0:T(4,128)S(1)}, f32[3,256]{1,0:T(4,128)S(1)}, u32[]{:S(2)}, u32[]{:S(2)}) collective-permute-start(f32[3,256]{1,0:T(4,128)S(1)} %add.322), channel_id=1, source_target_pairs={{0,16},{16,32},{32,48},{48,64},{64,80},{80,96},{96,112},{112,128},... | collective-permute-start | bytes 9224 | tf_op jit(solution)/shard_map/while/body/eval_jaxpr/ppermute | solution.py:17
  284.0 7.7 %collective-permute-start = (f32[3,256]{1,0:T(4,128)S(1)}, f32[3,256]{1,0:T(4,128)S(1)}, u32[]{:S(2)}, u32[]{:S(2)}) collective-permute-start(f32[3,256]{1,0:T(4,128)S(1)} %add.322), channel_id=1, source_target_pairs={{0,16},{16,32},{32,48},{48,64},{64,80},{80,96},{96,112},{112,128},... | collective-permute-start | bytes 9224 | tf_op jit(solution)/shard_map/while/body/eval_jaxpr/ppermute | solution.py:17
  291.7 7.7 %collective-permute-start = (f32[3,256]{1,0:T(4,128)S(1)}, f32[3,256]{1,0:T(4,128)S(1)}, u32[]{:S(2)}, u32[]{:S(2)}) collective-permute-start(f32[3,256]{1,0:T(4,128)S(1)} %add.322), channel_id=1, source_target_pairs={{0,16},{16,32},{32,48},{48,64},{64,80},{80,96},{96,112},{112,128},... | collective-permute-start | bytes 9224 | tf_op jit(solution)/shard_map/while/body/eval_jaxpr/ppermute | solution.py:17
  299.3 7.7 %collective-permute-start = (f32[3,256]{1,0:T(4,128)S(1)}, f32[3,256]{1,0:T(4,128)S(1)}, u32[]{:S(2)}, u32[]{:S(2)}) collective-permute-start(f32[3,256]{1,0:T(4,128)S(1)} %add.322), channel_id=1, source_target_pairs={{0,16},{16,32},{32,48},{48,64},{64,80},{80,96},{96,112},{112,128},... | collective-permute-start | bytes 9224 | tf_op jit(solution)/shard_map/while/body/eval_jaxpr/ppermute | solution.py:17
  307.0 7.7 %collective-permute-start = (f32[3,256]{1,0:T(4,128)S(1)}, f32[3,256]{1,0:T(4,128)S(1)}, u32[]{:S(2)}, u32[]{:S(2)}) collective-permute-start(f32[3,256]{1,0:T(4,128)S(1)} %add.322), channel_id=1, source_target_pairs={{0,16},{16,32},{32,48},{48,64},{64,80},{80,96},{96,112},{112,128},... | collective-permute-start | bytes 9224 | tf_op jit(solution)/shard_map/while/body/eval_jaxpr/ppermute | solution.py:17
  314.7 7.7 %collective-permute-start = (f32[3,256]{1,0:T(4,128)S(1)}, f32[3,256]{1,0:T(4,128)S(1)}, u32[]{:S(2)}, u32[]{:S(2)}) collective-permute-start(f32[3,256]{1,0:T(4,128)S(1)} %add.322), channel_id=1, source_target_pairs={{0,16},{16,32},{32,48},{48,64},{64,80},{80,96},{96,112},{112,128},... | collective-permute-start | bytes 9224 | tf_op jit(solution)/shard_map/while/body/eval_jaxpr/ppermute | solution.py:17
  322.4 7.7 %collective-permute-start = (f32[3,256]{1,0:T(4,128)S(1)}, f32[3,256]{1,0:T(4,128)S(1)}, u32[]{:S(2)}, u32[]{:S(2)}) collective-permute-start(f32[3,256]{1,0:T(4,128)S(1)} %add.322), channel_id=1, source_target_pairs={{0,16},{16,32},{32,48},{48,64},{64,80},{80,96},{96,112},{112,128},... | collective-permute-start | bytes 9224 | tf_op jit(solution)/shard_map/while/body/eval_jaxpr/ppermute | solution.py:17
  330.1 7.7 %collective-permute-start = (f32[3,256]{1,0:T(4,128)S(1)}, f32[3,256]{1,0:T(4,128)S(1)}, u32[]{:S(2)}, u32[]{:S(2)}) collective-permute-start(f32[3,256]{1,0:T(4,128)S(1)} %add.322), channel_id=1, source_target_pairs={{0,16},{16,32},{32,48},{48,64},{64,80},{80,96},{96,112},{112,128},... | collective-permute-start | bytes 9224 | tf_op jit(solution)/shard_map/while/body/eval_jaxpr/ppermute | solution.py:17
  337.7 7.7 %collective-permute-start = (f32[3,256]{1,0:T(4,128)S(1)}, f32[3,256]{1,0:T(4,128)S(1)}, u32[]{:S(2)}, u32[]{:S(2)}) collective-permute-start(f32[3,256]{1,0:T(4,128)S(1)} %add.322), channel_id=1, source_target_pairs={{0,16},{16,32},{32,48},{48,64},{64,80},{80,96},{96,112},{112,128},... | collective-permute-start | bytes 9224 | tf_op jit(solution)/shard_map/while/body/eval_jaxpr/ppermute | solution.py:17
  345.4 7.7 %collective-permute-start = (f32[3,256]{1,0:T(4,128)S(1)}, f32[3,256]{1,0:T(4,128)S(1)}, u32[]{:S(2)}, u32[]{:S(2)}) collective-permute-start(f32[3,256]{1,0:T(4,128)S(1)} %add.322), channel_id=1, source_target_pairs={{0,16},{16,32},{32,48},{48,64},{64,80},{80,96},{96,112},{112,128},... | collective-permute-start | bytes 9224 | tf_op jit(solution)/shard_map/while/body/eval_jaxpr/ppermute | solution.py:17
  353.1 7.7 %collective-permute-start = (f32[3,256]{1,0:T(4,128)S(1)}, f32[3,256]{1,0:T(4,128)S(1)}, u32[]{:S(2)}, u32[]{:S(2)}) collective-permute-start(f32[3,256]{1,0:T(4,128)S(1)} %add.322), channel_id=1, source_target_pairs={{0,16},{16,32},{32,48},{48,64},{64,80},{80,96},{96,112},{112,128},... | collective-permute-start | bytes 9224 | tf_op jit(solution)/shard_map/while/body/eval_jaxpr/ppermute | solution.py:17
  360.8 7.7 %collective-permute-start = (f32[3,256]{1,0:T(4,128)S(1)}, f32[3,256]{1,0:T(4,128)S(1)}, u32[]{:S(2)}, u32[]{:S(2)}) collective-permute-start(f32[3,256]{1,0:T(4,128)S(1)} %add.322), channel_id=1, source_target_pairs={{0,16},{16,32},{32,48},{48,64},{64,80},{80,96},{96,112},{112,128},... | collective-permute-start | bytes 9224 | tf_op jit(solution)/shard_map/while/body/eval_jaxpr/ppermute | solution.py:17
  368.4 7.7 %collective-permute-start = (f32[3,256]{1,0:T(4,128)S(1)}, f32[3,256]{1,0:T(4,128)S(1)}, u32[]{:S(2)}, u32[]{:S(2)}) collective-permute-start(f32[3,256]{1,0:T(4,128)S(1)} %add.322), channel_id=1, source_target_pairs={{0,16},{16,32},{32,48},{48,64},{64,80},{80,96},{96,112},{112,128},... | collective-permute-start | bytes 9224 | tf_op jit(solution)/shard_map/while/body/eval_jaxpr/ppermute | solution.py:17
  376.1 7.7 %collective-permute-start = (f32[3,256]{1,0:T(4,128)S(1)}, f32[3,256]{1,0:T(4,128)S(1)}, u32[]{:S(2)}, u32[]{:S(2)}) collective-permute-start(f32[3,256]{1,0:T(4,128)S(1)} %add.322), channel_id=1, source_target_pairs={{0,16},{16,32},{32,48},{48,64},{64,80},{80,96},{96,112},{112,128},... | collective-permute-start | bytes 9224 | tf_op jit(solution)/shard_map/while/body/eval_jaxpr/ppermute | solution.py:17
  383.8 7.7 %collective-permute-start = (f32[3,256]{1,0:T(4,128)S(1)}, f32[3,256]{1,0:T(4,128)S(1)}, u32[]{:S(2)}, u32[]{:S(2)}) collective-permute-start(f32[3,256]{1,0:T(4,128)S(1)} %add.322), channel_id=1, source_target_pairs={{0,16},{16,32},{32,48},{48,64},{64,80},{80,96},{96,112},{112,128},... | collective-permute-start | bytes 9224 | tf_op jit(solution)/shard_map/while/body/eval_jaxpr/ppermute | solution.py:17
  391.4 7.7 %collective-permute-start = (f32[3,256]{1,0:T(4,128)S(1)}, f32[3,256]{1,0:T(4,128)S(1)}, u32[]{:S(2)}, u32[]{:S(2)}) collective-permute-start(f32[3,256]{1,0:T(4,128)S(1)} %add.322), channel_id=1, source_target_pairs={{0,16},{16,32},{32,48},{48,64},{64,80},{80,96},{96,112},{112,128},... | collective-permute-start | bytes 9224 | tf_op jit(solution)/shard_map/while/body/eval_jaxpr/ppermute | solution.py:17
  399.1 7.7 %collective-permute-start = (f32[3,256]{1,0:T(4,128)S(1)}, f32[3,256]{1,0:T(4,128)S(1)}, u32[]{:S(2)}, u32[]{:S(2)}) collective-permute-start(f32[3,256]{1,0:T(4,128)S(1)} %add.322), channel_id=1, source_target_pairs={{0,16},{16,32},{32,48},{48,64},{64,80},{80,96},{96,112},{112,128},... | collective-permute-start | bytes 9224 | tf_op jit(solution)/shard_map/while/body/eval_jaxpr/ppermute | solution.py:17
  406.8 7.7 %collective-permute-start = (f32[3,256]{1,0:T(4,128)S(1)}, f32[3,256]{1,0:T(4,128)S(1)}, u32[]{:S(2)}, u32[]{:S(2)}) collective-permute-start(f32[3,256]{1,0:T(4,128)S(1)} %add.322), channel_id=1, source_target_pairs={{0,16},{16,32},{32,48},{48,64},{64,80},{80,96},{96,112},{112,128},... | collective-permute-start | bytes 9224 | tf_op jit(solution)/shard_map/while/body/eval_jaxpr/ppermute | solution.py:17
  414.5 7.7 %collective-permute-start = (f32[3,256]{1,0:T(4,128)S(1)}, f32[3,256]{1,0:T(4,128)S(1)}, u32[]{:S(2)}, u32[]{:S(2)}) collective-permute-start(f32[3,256]{1,0:T(4,128)S(1)} %add.322), channel_id=1, source_target_pairs={{0,16},{16,32},{32,48},{48,64},{64,80},{80,96},{96,112},{112,128},... | collective-permute-start | bytes 9224 | tf_op jit(solution)/shard_map/while/body/eval_jaxpr/ppermute | solution.py:17
  422.1 7.7 %collective-permute-start = (f32[3,256]{1,0:T(4,128)S(1)}, f32[3,256]{1,0:T(4,128)S(1)}, u32[]{:S(2)}, u32[]{:S(2)}) collective-permute-start(f32[3,256]{1,0:T(4,128)S(1)} %add.322), channel_id=1, source_target_pairs={{0,16},{16,32},{32,48},{48,64},{64,80},{80,96},{96,112},{112,128},... | collective-permute-start | bytes 9224 | tf_op jit(solution)/shard_map/while/body/eval_jaxpr/ppermute | solution.py:17
  429.8 7.7 %collective-permute-start = (f32[3,256]{1,0:T(4,128)S(1)}, f32[3,256]{1,0:T(4,128)S(1)}, u32[]{:S(2)}, u32[]{:S(2)}) collective-permute-start(f32[3,256]{1,0:T(4,128)S(1)} %add.322), channel_id=1, source_target_pairs={{0,16},{16,32},{32,48},{48,64},{64,80},{80,96},{96,112},{112,128},... | collective-permute-start | bytes 9224 | tf_op jit(solution)/shard_map/while/body/eval_jaxpr/ppermute | solution.py:17
  437.5 7.7 %collective-permute-start = (f32[3,256]{1,0:T(4,128)S(1)}, f32[3,256]{1,0:T(4,128)S(1)}, u32[]{:S(2)}, u32[]{:S(2)}) collective-permute-start(f32[3,256]{1,0:T(4,128)S(1)} %add.322), channel_id=1, source_target_pairs={{0,16},{16,32},{32,48},{48,64},{64,80},{80,96},{96,112},{112,128},... | collective-permute-start | bytes 9224 | tf_op jit(solution)/shard_map/while/body/eval_jaxpr/ppermute | solution.py:17
  (10 other events, 176.7 us)
Sparse Core Ops, SparseCore 0:
  213.4 53.6 reduce-scatter.1
where the time goes:
time: 578 us; the launch traced here: 573 us
  waiting for transfers between devices  231 us (40%)
  matrix products  115 us (20%)
  blocking collectives  111 us (19%)
  starting transfers between devices  60.6 us (10%)
  other arithmetic  34.2 us (6%)
  between operations  14.2 us (2%)
    ppermute x31, waiting for transfers between devices, passed_along(): return lax.ppermute(block, axis, route)  177 us
    dot_general x40, matrix products, pair_field(): jnp.einsum('ts,cs->ct', kernel, moments, precision=lax.Precision.HIGHEST)  108 us
    ppermute x31, starting transfers between devices, passed_along(): return lax.ppermute(block, axis, route)  60.5 us
    all_gather x1, blocking collectives, body(): window = lax.all_gather(correction, 'dom', axis=1, tiled=True)  54 us
    reduce_scatter x1, waiting for transfers between devices, body(): lax.psum_scatter(partial_value, 'dom', scatter_dimension=1, tiled=True)  53.9 us
    all_gather x2, blocking collectives, swept_field(): lax.all_gather(stacked, 'dom', axis=2, tiled=True)  31.9 us
    reduce_sum x32, other arithmetic, pair_field(): radius_sq = jnp.sum(offsets * offsets, axis=0) + sigma_sq  29.4 us
    all_gather x1, blocking collectives, body(): lax.all_gather(stacked, 'dom', axis=2, tiled=True)  25.1 us
  transfers between devices with their start and end apart: 32, of which 32 were waited for; matrix products, arithmetic and copies ran while one was open for 0% of the time, Pallas kernels for 0%

commit v1 on v0

v1 whole, which is shorter than its diff:
```python
import math

import jax
import jax.numpy as jnp
from jax import lax
from jax.experimental import pallas as pl
from jax.experimental.pallas import tpu as pltpu
from jax.sharding import PartitionSpec as P

f32 = jnp.float32
bf16 = jnp.bfloat16
inv_four_pi = 1.0 / (4.0 * math.pi)
sigma_sq = 0.01
dt_slice = 0.5
node_weights = ((5.0 / 24.0, 1.0 / 3.0, -1.0 / 24.0), (-1.0 / 24.0, 1.0 / 3.0, 5.0 / 24.0))
vmem_bytes = 52 << 20
source_rows = 18
moment_rows = 16


def high_part(value):
    return value.astype(bf16).astype(f32)


def parts_of(value, number):
    found = []
    for _ in range(number - 1):
        high = high_part(value)
        found.append(high)
        value = value - high
    found.append(high_part(value))
    return found


def norm_sq(rows):
    return rows[0:1] * rows[0:1] + rows[1:2] * rows[1:2] + rows[2:3] * rows[2:3]


def cross(a, b):
    return jnp.concatenate(
        [
            a[1:2] * b[2:3] - a[2:3] * b[1:2],
            a[2:3] * b[0:1] - a[0:1] * b[2:3],
            a[0:1] * b[1:2] - a[1:2] * b[0:1],
        ],
        0,
    )


def source_features(p):
    high, low = parts_of(p, 2)
    sq = parts_of(norm_sq(high + low), 3)
    one = jnp.ones_like(sq[0])
    return jnp.concatenate([high, high, low, low, *sq, one, one, one], 0).astype(bf16)


def target_features(x):
    high, low = parts_of(x, 2)
    sq = parts_of(norm_sq(high + low) + sigma_sq, 3)
    one = jnp.ones_like(sq[0])
    rows = [-2.0 * high, -2.0 * low, -2.0 * high, -2.0 * low, one, one, one, *sq]
    return jnp.concatenate(rows, 0).astype(bf16)


def source_moments(p, w):
    w = w * inv_four_pi
    pad = jnp.zeros((moment_rows - 12, p.shape[1]), f32)
    return jnp.concatenate([*parts_of(w, 2), *parts_of(cross(w, p), 2), pad], 0).astype(bf16)


def field(blocks, x, center, features, moments):
    width = x.shape[1]
    for number, (p, w) in enumerate(blocks):
        lanes = pl.ds(number * width, width)
        shifted = p - center
        features[:, lanes] = source_features(shifted)
        moments[:, lanes] = source_moments(shifted, w)
    x = x - center
    sq = lax.dot_general(
        features[...], target_features(x), (((0,), (0,)), ((), ())), preferred_element_type=f32
    )
    root = lax.rsqrt(sq)
    kernel = (root * root * root).astype(bf16)
    summed = jnp.dot(moments[...], kernel, preferred_element_type=f32)
    return cross(summed[0:3] + summed[3:6], x) - (summed[6:9] + summed[9:12])


def quad(row, a, b, c):
    return dt_slice * (row[0] * a + row[1] * b + row[2] * c)


def spread_out(ref, value):
    for number in range(ref.shape[0]):
        ref[number] = value


def nodes_kernel(all_ref, own_ref, velocity_ref, second_ref, send_ref, features, moments):
    halves, lines = all_ref.shape[:2]
    center = own_ref[0:3, 0:1]
    found = []
    for node in range(3):
        rows = pl.ds(3 * node, 3)
        blocks = [
            (all_ref[h, z, rows], all_ref[h, z, 9:12]) for z in range(lines) for h in range(halves)
        ]
        found.append(field(blocks, own_ref[rows], center, features, moments))
    velocity_ref[...] = jnp.concatenate(found, 0)
    second = own_ref[0:3] + quad(node_weights[0], *found)
    second_ref[...] = second
    spread_out(send_ref, second)


def swept_blocks(all_ref, gathered_ref):
    halves, lines = all_ref.shape[:2]
    return [
        (gathered_ref[halves * z + h], all_ref[h, z, 9:12])
        for z in range(lines)
        for h in range(halves)
    ]


def second_kernel(
    all_ref, gathered_ref, velocity_ref, second_ref, swept_ref, third_ref, send_ref, features, moments
):
    second = second_ref[...]
    blocks = swept_blocks(all_ref, gathered_ref)
    swept = field(blocks, second, second[:, 0:1], features, moments)
    swept_ref[...] = swept
    nodes = [velocity_ref[pl.ds(3 * node, 3)] for node in range(3)]
    third = second + 0.5 * dt_slice * (swept - nodes[1]) + quad(node_weights[1], *nodes)
    third_ref[...] = third
    spread_out(send_ref, third)


def third_kernel(
    all_ref, gathered_ref, velocity_ref, swept_ref, third_ref, send_ref, features, moments
):
    third = third_ref[...]
    blocks = swept_blocks(all_ref, gathered_ref)
    last = field(blocks, third, third[:, 0:1], features, moments)
    early = quad(node_weights[0], velocity_ref[0:3], swept_ref[...], last)
    late = quad(node_weights[1], velocity_ref[0:3], swept_ref[...], last)
    spread_out(send_ref, jnp.concatenate([early, early + late], 0))


def means_kernel(all_ref, second_ref, third_ref, quads_ref, coarse_ref, means_ref, send_ref, rows):
    halves, lines = all_ref.shape[:2]
    width = coarse_ref.shape[1]
    mine = jnp.broadcast_to(coarse_ref[...], (8, width)).T[:, 0:1]
    total = jnp.zeros((rows.shape[0], width), f32)
    for z in range(lines):
        for h in range(halves):
            number = halves * z + h
            values = jnp.concatenate(
                [all_ref[h, z, 0:3], second_ref[number], third_ref[number], quads_ref[number]], 0
            )
            ones = jnp.ones((3, width), f32)
            rows[...] = jnp.concatenate([*parts_of(values, 3), ones], 0).astype(bf16)
            same = jnp.where(mine == all_ref[h, z, 12:13], 1.0, 0.0).astype(bf16)
            total = total + lax.dot_general(
                rows[...], same, (((1,), (1,)), ((), ())), preferred_element_type=f32
            )
    means = (total[0:15] + total[15:30] + total[30:45]) / total[45:46]
    means_ref[...] = means
    first_slice = lax.axis_index("tm") == 0
    spread_out(send_ref, means[12:15] + jnp.where(first_slice, means[0:3], 0.0))


def ends_kernel(received_ref, means_ref, own_ref, second_ref, third_ref, fine_ref, end_ref):
    slice_index = lax.axis_index("tm")
    begin = jnp.where(slice_index == 0, means_ref[0:3], 0.0)
    for number in range(received_ref.shape[0]):
        begin = begin + jnp.where(number < slice_index, received_ref[number], 0.0)
    finish = begin + means_ref[12:15]
    fine_ref[0:3] = own_ref[0:3] + (begin - means_ref[0:3])
    fine_ref[3:6] = second_ref[...] + ((begin + means_ref[9:12]) - means_ref[3:6])
    fine_ref[6:9] = third_ref[...] + (finish - means_ref[6:9])
    width, half = finish.shape[1], end_ref.shape[1]
    even = lax.broadcasted_iota(jnp.int32, (width, half), 0) == 2 * lax.broadcasted_iota(
        jnp.int32, (width, half), 1
    )
    pick = jnp.where(even, 1.0, 0.0).astype(bf16)
    stacked = jnp.concatenate(parts_of(finish, 3), 0).astype(bf16)
    picked = jnp.dot(stacked, pick, preferred_element_type=f32)
    end_ref[...] = picked[0:3] + picked[3:6] + picked[6:9]


def call(kernel, shapes, scratch, *operands):
    return pl.pallas_call(
        kernel,
        out_shape=[jax.ShapeDtypeStruct(shape, f32) for shape in shapes],
        scratch_shapes=[pltpu.VMEM(shape, bf16) for shape in scratch],
        compiler_params=pltpu.CompilerParams(vmem_limit_bytes=vmem_bytes),
    )(*operands)


def body(node_pos, vorticity, coarse_of):
    width = vorticity.shape[1]
    domains = lax.axis_size("dom")
    slices = lax.axis_size("tm")
    own = node_pos.reshape(9, width)
    coarse = coarse_of.astype(f32)[None]
    block = jnp.concatenate([own, vorticity, coarse], 0)
    lines = domains // 2
    same_core = [[2 * z + h for z in range(lines)] for h in range(2)]
    same_chip = [[2 * z, 2 * z + 1] for z in range(lines)]
    along = lax.all_to_all(
        jnp.broadcast_to(block[None], (lines,) + block.shape),
        "dom",
        0,
        0,
        axis_index_groups=same_core,
    )
    everyone = lax.all_gather(along, "dom", axis=0, axis_index_groups=same_chip)
    count = domains * width
    scratch = [(source_rows, count), (moment_rows, count)]
    three = (3, width)
    velocity, second, send = call(
        nodes_kernel, [(9, width), three, (domains,) + three], scratch, everyone, own
    )
    seconds = lax.all_to_all(send, "dom", 0, 0)
    swept, third, send = call(
        second_kernel,
        [three, three, (domains,) + three],
        scratch,
        everyone,
        seconds,
        velocity,
        second,
    )
    thirds = lax.all_to_all(send, "dom", 0, 0)
    (send,) = call(
        third_kernel, [(domains, 6, width)], scratch, everyone, thirds, velocity, swept, third
    )
    quads = lax.all_to_all(send, "dom", 0, 0)
    means, send = call(
        means_kernel,
        [(15, width), (slices,) + three],
        [(48, width)],
        everyone,
        seconds,
        thirds,
        quads,
        coarse,
    )
    received = lax.all_to_all(send, "tm", 0, 0)
    fine_nodes, coarse_end = call(
        ends_kernel, [(9, width), (3, width // 2)], [], received, means, own, second, third
    )
    return fine_nodes.reshape(node_pos.shape), coarse_end[None]


def solution(mesh):
    return jax.shard_map(
        body,
        mesh=mesh,
        in_specs=(P("tm", None, None, "dom"), P(None, "dom"), P("dom")),
        out_specs=(P("tm", None, None, "dom"), P("tm", None, "dom")),
        check_vma=False,
    )
```

time: 578 us -> 113 us (0.20)
  the two profiles are of different devices: /device:TPU:33 before, /device:TPU:1 now
where the time goes in v1:
time: 113 us
  blocking collectives  84.9 us (75%)
  Pallas kernels  23.6 us (21%)
  local copies, waits for them, and re-layouts  2.3 us (2%)
  other arithmetic  1.47 us (1%)
    pallas_call x5, Pallas kernels, call(): pl.pallas_call(kernel, out_shape=[jax.ShapeDtypeStruct(shape, f32) for sh...  23.6 us
    all_to_all x1, blocking collectives, body(): received = lax.all_to_all(send, 'tm', 0, 0)  22 us
    all_to_all x1, blocking collectives, body(): lax.all_to_all(jnp.broadcast_to(block[None], (lines,) + block.shape), 'do...  21 us
    all_to_all x1, blocking collectives, body(): quads = lax.all_to_all(send, 'dom', 0, 0)  14.1 us
    all_to_all x1, blocking collectives, body(): seconds = lax.all_to_all(send, 'dom', 0, 0)  12 us
    all_to_all x1, blocking collectives, body(): thirds = lax.all_to_all(send, 'dom', 0, 0)  11.6 us
    all_gather x1, blocking collectives, body(): everyone = lax.all_gather(along, 'dom', axis=0, axis_index_groups=same_chip)  4.2 us

profile of v1, /device:TPU:1, one launch (start us, length us, event | category | flops | bytes accessed | tf_op | source)
XLA Modules:
  0.0 113.0 jit_solution(12222952993457872474)
XLA Ops:
  0.6 0.7 convert_element_type.3
  1.3 0.8 reduce
  2.1 0.0 copy-start
  2.1 0.7 copy-done
  2.8 21.0 %all_to_all.25 = f32[8,13,512]{2,1,0:T(8,128)S(1)} all-to-all(f32[8,13,512]{2,1,0:T(8,128)S(1)} %broadcast_in_dim.13), channel_id=1, replica_groups={{0,2,4,6,8,10,12,14},{1,3,5,7,9,11,13,15},{16,18,20,22,24,26,28,30},{17..., dimensions={0} | all-to-all | bytes 425984 | tf_op jit(solution)/shard_map/all_to_all | solution.py:207
  23.9 0.1 copy.12
  24.0 4.2 %all-gather = f32[16,13,512]{2,0,1:T(8,128)S(1)} all-gather(f32[8,13,512]{2,0,1:T(8,128)S(1)} %copy.12), channel_id=2, replica_groups={{0,1},{2,3},{4,5},{6,7},{8,9},{10,11},{12,13},{14,15},{16,17},{18,19},{..., dimensions={0}, use_global_device_ids=true | all-gather | bytes 638976 | tf_op jit(solution)/shard_map/all_gather | solution.py:214
  28.2 0.3 copy.13
  28.5 12.2 %shard_map.50 = (f32[9,512]{1,0:T(8,128)S(1)}, f32[3,512]{1,0:T(4,128)S(1)}, f32[16,3,512]{2,1,0:T(4,128)S(1)}) custom-call(f32[2,8,13,512]{3,2,1,0:T(8,128)S(1)} %bitcast.3, f32[9,512]{1,0:T(8,128)S(1)} %reshape.11.own_ref), custom_call_target="tpu_custom_call" | custom-call | tf_op jit(solution)/shard_map/pallas_call | solution.py:189
  40.7 12.0 %all_to_all.26.gathered_ref.second_ref = f32[16,3,512]{2,1,0:T(4,128)S(1)} all-to-all(f32[16,3,512]{2,1,0:T(4,128)S(1)} %get-tuple-element.12), channel_id=1, replica_groups=mesh['tm'=32,'dom'=16] {'dom'}, dimensions={0} | all-to-all | bytes 196608 | tf_op jit(solution)/shard_map/all_to_all | solution.py:221
  52.7 4.1 %shard_map.51 = (f32[3,512]{1,0:T(4,128)S(1)}, f32[3,512]{1,0:T(4,128)S(1)}, f32[16,3,512]{2,1,0:T(4,128)S(1)}) custom-call(f32[2,8,13,512]{3,2,1,0:T(8,128)S(1)} %bitcast.4, f32[16,3,512]{2,1,0:T(4,128)S(1)} %all_to_all.26.gathered_ref.second_ref, f32[9,512]{1,0:T(8,128)S(1)} %get-tuple-element.13.velocity_ref, f32[3,512]{1,0:T(4,128)S(1)} %get-tuple-element.14.second_ref), custom_call_target="tpu_custom_call" | custom-call | tf_op jit(solution)/shard_map/pallas_call | solution.py:189
  56.8 11.6 %all_to_all.27.gathered_ref.third_ref = f32[16,3,512]{2,1,0:T(4,128)S(1)} all-to-all(f32[16,3,512]{2,1,0:T(4,128)S(1)} %get-tuple-element.15), channel_id=1, replica_groups=mesh['tm'=32,'dom'=16] {'dom'}, dimensions={0} | all-to-all | bytes 196608 | tf_op jit(solution)/shard_map/all_to_all | solution.py:231
  68.4 4.1 %shard_map.52 = f32[16,6,512]{2,1,0:T(8,128)S(1)} custom-call(f32[2,8,13,512]{3,2,1,0:T(8,128)S(1)} %bitcast.5, f32[16,3,512]{2,1,0:T(4,128)S(1)} %all_to_all.27.gathered_ref.third_ref, f32[9,512]{1,0:T(8,128)S(1)} %get-tuple-element.13.velocity_ref, f32[3,512]{1,0:T(4,128)S(1)} %get-tuple-element.16.swept_ref, f32[3,512]{1,0:T(4,128)S(1)} %get-tuple-element.17.third_ref), custom_call_target="tpu_custom_call" | custom-call | tf_op jit(solution)/shard_map/pallas_call | solution.py:189
  72.5 14.1 %all_to_all.28.quads_ref = f32[16,6,512]{2,1,0:T(8,128)S(1)} all-to-all(f32[16,6,512]{2,1,0:T(8,128)S(1)} %shard_map.52), channel_id=1, replica_groups=mesh['tm'=32,'dom'=16] {'dom'}, dimensions={0} | all-to-all | bytes 393216 | tf_op jit(solution)/shard_map/all_to_all | solution.py:235
  86.6 2.9 %shard_map.53 = (f32[15,512]{1,0:T(8,128)S(1)}, f32[32,3,512]{2,1,0:T(4,128)S(1)}) custom-call(f32[2,8,13,512]{3,2,1,0:T(8,128)S(1)} %bitcast.6, f32[16,3,512]{2,1,0:T(4,128)S(1)} %all_to_all.26.gathered_ref.second_ref, f32[16,3,512]{2,1,0:T(4,128)S(1)} %all_to_all.27.gathered_ref.third_ref, f32[16,6,512]{2,1,0:T(8,128)S(1)} %all_to_all.28.quads_ref, ...), custom_call_target="tpu_custom_call" | custom-call | tf_op jit(solution)/shard_map/pallas_call | solution.py:189
  89.6 22.0 %all_to_all.29.received_ref = f32[32,3,512]{2,1,0:T(4,128)S(1)} all-to-all(f32[32,3,512]{2,1,0:T(4,128)S(1)} %get-tuple-element.18), channel_id=1, replica_groups=mesh['tm'=32,'dom'=16] {'tm'}, dimensions={0} | all-to-all | bytes 393216 | tf_op jit(solution)/shard_map/all_to_all | solution.py:246
  111.5 0.2 shard_map.54
  111.7 0.6 reshape.14
  112.4 0.6 copy.15
  (3 shorter events, 0.0 us)
Async XLA Ops:
  2.1 0.7 copy-start

commit v2 on v1

--- a/solution.py
+++ b/solution.py
@@ -89,9 +89,29 @@
     return dt_slice * (row[0] * a + row[1] * b + row[2] * c)
 
 
+lane = 128
+
+
+def wide(ref, *index):
+    return jnp.concatenate([ref[(*index, chunk)] for chunk in range(ref.shape[-2])], 1)
+
+
+def store_chunks(ref, value):
+    for chunk in range(ref.shape[-2]):
+        ref[:, chunk] = value[:, chunk * lane : (chunk + 1) * lane]
+
+
 def spread_out(ref, value):
     for number in range(ref.shape[0]):
-        ref[number] = value
+        store_chunks(ref.at[number], value)
+
+
+def prepare_kernel(nodes_ref, vorticity_ref, coarse_ref, own_ref, mine_ref, send_ref):
+    own = nodes_ref[:, 0]
+    mine = coarse_ref[...].astype(f32)
+    own_ref[...] = own
+    mine_ref[...] = mine
+    spread_out(send_ref, jnp.concatenate([own, vorticity_ref[...], mine], 0))
 
 
 def nodes_kernel(all_ref, own_ref, velocity_ref, second_ref, send_ref, features, moments):
@@ -101,7 +121,9 @@
     for node in range(3):
         rows = pl.ds(3 * node, 3)
         blocks = [
-            (all_ref[h, z, rows], all_ref[h, z, 9:12]) for z in range(lines) for h in range(halves)
+            (wide(all_ref, h, z, rows), wide(all_ref, h, z, pl.ds(9, 3)))
+            for z in range(lines)
+            for h in range(halves)
         ]
         found.append(field(blocks, own_ref[rows], center, features, moments))
     velocity_ref[...] = jnp.concatenate(found, 0)
@@ -113,7 +135,7 @@
 def swept_blocks(all_ref, gathered_ref):
     halves, lines = all_ref.shape[:2]
     return [
-        (gathered_ref[halves * z + h], all_ref[h, z, 9:12])
+        (wide(gathered_ref, halves * z + h, pl.ds(0, 3)), wide(all_ref, h, z, pl.ds(9, 3)))
         for z in range(lines)
         for h in range(halves)
     ]
@@ -140,23 +162,38 @@
     last = field(blocks, third, third[:, 0:1], features, moments)
     early = quad(node_weights[0], velocity_ref[0:3], swept_ref[...], last)
     late = quad(node_weights[1], velocity_ref[0:3], swept_ref[...], last)
-    spread_out(send_ref, jnp.concatenate([early, early + late], 0))
+    chunks = early.shape[1] // lane
+    for number in range(send_ref.shape[0]):
+        for chunk in range(chunks):
+            lanes = slice(chunk * lane, (chunk + 1) * lane)
+            send_ref[number, :, chunk] = early[:, lanes]
+            send_ref[number, :, chunks + chunk] = (early + late)[:, lanes]
 
 
 def means_kernel(all_ref, second_ref, third_ref, quads_ref, coarse_ref, means_ref, send_ref, rows):
     halves, lines = all_ref.shape[:2]
     width = coarse_ref.shape[1]
+    chunks = width // lane
     mine = jnp.broadcast_to(coarse_ref[...], (8, width)).T[:, 0:1]
     total = jnp.zeros((rows.shape[0], width), f32)
     for z in range(lines):
         for h in range(halves):
             number = halves * z + h
+            both = wide(quads_ref, number, pl.ds(0, 3))
             values = jnp.concatenate(
-                [all_ref[h, z, 0:3], second_ref[number], third_ref[number], quads_ref[number]], 0
+                [
+                    wide(all_ref, h, z, pl.ds(0, 3)),
+                    wide(second_ref, number, pl.ds(0, 3)),
+                    wide(third_ref, number, pl.ds(0, 3)),
+                    both[:, :width],
+                    both[:, width:],
+                ],
+                0,
             )
             ones = jnp.ones((3, width), f32)
             rows[...] = jnp.concatenate([*parts_of(values, 3), ones], 0).astype(bf16)
-            same = jnp.where(mine == all_ref[h, z, 12:13], 1.0, 0.0).astype(bf16)
+            theirs = wide(all_ref, h, z, pl.ds(12, 1))
+            same = jnp.where(mine == theirs, 1.0, 0.0).astype(bf16)
             total = total + lax.dot_general(
                 rows[...], same, (((1,), (1,)), ((), ())), preferred_element_type=f32
             )
@@ -168,21 +205,23 @@
 
 def ends_kernel(received_ref, means_ref, own_ref, second_ref, third_ref, fine_ref, end_ref):
     slice_index = lax.axis_index("tm")
-    begin = jnp.where(slice_index == 0, means_ref[0:3], 0.0)
+    gathered = jnp.zeros(received_ref.shape[1:], f32)
     for number in range(received_ref.shape[0]):
-        begin = begin + jnp.where(number < slice_index, received_ref[number], 0.0)
+        gathered = gathered + jnp.where(number < slice_index, received_ref[number], 0.0)
+    gathered = jnp.concatenate([gathered[:, chunk] for chunk in range(gathered.shape[1])], 1)
+    begin = jnp.where(slice_index == 0, means_ref[0:3], gathered)
     finish = begin + means_ref[12:15]
-    fine_ref[0:3] = own_ref[0:3] + (begin - means_ref[0:3])
-    fine_ref[3:6] = second_ref[...] + ((begin + means_ref[9:12]) - means_ref[3:6])
-    fine_ref[6:9] = third_ref[...] + (finish - means_ref[6:9])
-    width, half = finish.shape[1], end_ref.shape[1]
+    fine_ref[0:3, 0] = own_ref[0:3] + (begin - means_ref[0:3])
+    fine_ref[3:6, 0] = second_ref[...] + ((begin + means_ref[9:12]) - means_ref[3:6])
+    fine_ref[6:9, 0] = third_ref[...] + (finish - means_ref[6:9])
+    width, half = finish.shape[1], end_ref.shape[2]
     even = lax.broadcasted_iota(jnp.int32, (width, half), 0) == 2 * lax.broadcasted_iota(
         jnp.int32, (width, half), 1
     )
     pick = jnp.where(even, 1.0, 0.0).astype(bf16)
     stacked = jnp.concatenate(parts_of(finish, 3), 0).astype(bf16)
     picked = jnp.dot(stacked, pick, preferred_element_type=f32)
-    end_ref[...] = picked[0:3] + picked[3:6] + picked[6:9]
+    end_ref[:, 0] = picked[0:3] + picked[3:6] + picked[6:9]
 
 
 def call(kernel, shapes, scratch, *operands):
@@ -198,30 +237,31 @@
     width = vorticity.shape[1]
     domains = lax.axis_size("dom")
     slices = lax.axis_size("tm")
-    own = node_pos.reshape(9, width)
-    coarse = coarse_of.astype(f32)[None]
-    block = jnp.concatenate([own, vorticity, coarse], 0)
     lines = domains // 2
+    chunks = width // lane
     same_core = [[2 * z + h for z in range(lines)] for h in range(2)]
     same_chip = [[2 * z, 2 * z + 1] for z in range(lines)]
-    along = lax.all_to_all(
-        jnp.broadcast_to(block[None], (lines,) + block.shape),
-        "dom",
-        0,
-        0,
-        axis_index_groups=same_core,
-    )
+    own, mine, send = call(
+        prepare_kernel,
+        [(9, width), (1, width), (lines, 13, chunks, lane)],
+        [],
+        node_pos.reshape(9, 1, width),
+        vorticity,
+        coarse_of[None],
+    )
+    along = lax.all_to_all(send, "dom", 0, 0, axis_index_groups=same_core)
     everyone = lax.all_gather(along, "dom", axis=0, axis_index_groups=same_chip)
     count = domains * width
     scratch = [(source_rows, count), (moment_rows, count)]
     three = (3, width)
+    packed = (3, chunks, lane)
     velocity, second, send = call(
-        nodes_kernel, [(9, width), three, (domains,) + three], scratch, everyone, own
+        nodes_kernel, [(9, width), three, (domains,) + packed], scratch, everyone, own
     )
     seconds = lax.all_to_all(send, "dom", 0, 0)
     swept, third, send = call(
         second_kernel,
-        [three, three, (domains,) + three],
+        [three, three, (domains,) + packed],
         scratch,
         everyone,
         seconds,
@@ -230,24 +270,38 @@
     )
     thirds = lax.all_to_all(send, "dom", 0, 0)
     (send,) = call(
-        third_kernel, [(domains, 6, width)], scratch, everyone, thirds, velocity, swept, third
+        third_kernel,
+        [(domains, 3, 2 * chunks, lane)],
+        scratch,
+        everyone,
+        thirds,
+        velocity,
+        swept,
+        third,
     )
     quads = lax.all_to_all(send, "dom", 0, 0)
     means, send = call(
         means_kernel,
-        [(15, width), (slices,) + three],
+        [(15, width), (slices,) + packed],
         [(48, width)],
         everyone,
         seconds,
         thirds,
         quads,
-        coarse,
+        mine,
     )
     received = lax.all_to_all(send, "tm", 0, 0)
     fine_nodes, coarse_end = call(
-        ends_kernel, [(9, width), (3, width // 2)], [], received, means, own, second, third
-    )
-    return fine_nodes.reshape(node_pos.shape), coarse_end[None]
+        ends_kernel,
+        [(9, 1, width), (3, 1, width // 2)],
+        [],
+        received,
+        means,
+        own,
+        second,
+        third,
+    )
+    return fine_nodes.reshape(node_pos.shape), coarse_end.reshape(1, 3, width // 2)
 
 
 def solution(mesh):

time: 113 us -> 108 us (0.956)
  blocking collectives: 84.9 us -> 79.5 us
  Pallas kernels: 23.6 us -> 25.1 us
  other arithmetic: 1.47 us -> 0 us
    all_to_all x1, blocking collectives: 22 us -> 20.5 us  [body(): received = lax.all_to_all(send, 'tm', 0, 0)]
    pallas_call x5 -> x6, Pallas kernels: 23.6 us -> 25.1 us  [call(): pl.pallas_call(kernel, out_shape=[jax.ShapeDtypeStruct(shape, f32) for sh...]
    all_to_all x1, blocking collectives: 14.1 us -> 12.7 us  [body(): quads = lax.all_to_all(send, 'dom', 0, 0)]
    all_to_all x1, blocking collectives: 21 us -> 19.7 us  [body(): along = lax.all_to_all(send, 'dom', 0, 0, axis_index_groups=same_core)]
where the time goes in v2:
time: 108 us; the launch traced here: 107 us
  blocking collectives  79.5 us (74%)
  Pallas kernels  25.1 us (23%)
  local copies, waits for them, and re-layouts  2.09 us (2%)
    pallas_call x6, Pallas kernels, call(): pl.pallas_call(kernel, out_shape=[jax.ShapeDtypeStruct(shape, f32) for sh...  25.1 us
    all_to_all x1, blocking collectives, body(): received = lax.all_to_all(send, 'tm', 0, 0)  20.5 us
    all_to_all x1, blocking collectives, body(): along = lax.all_to_all(send, 'dom', 0, 0, axis_index_groups=same_core)  19.7 us
    all_to_all x1, blocking collectives, body(): quads = lax.all_to_all(send, 'dom', 0, 0)  12.7 us
    all_to_all x1, blocking collectives, body(): seconds = lax.all_to_all(send, 'dom', 0, 0)  11.3 us
    all_to_all x1, blocking collectives, body(): thirds = lax.all_to_all(send, 'dom', 0, 0)  10.9 us
    all_gather x1, blocking collectives, body(): everyone = lax.all_gather(along, 'dom', axis=0, axis_index_groups=same_chip)  4.48 us

profile of v2, /device:TPU:1, one launch (start us, length us, event | category | flops | bytes accessed | tf_op | source)
XLA Modules:
  0.0 107.4 jit_solution(16598355926688529727)
XLA Ops:
  0.6 0.0 copy-start.2
  0.6 0.7 copy-done.2
  1.3 0.0 copy-start
  1.3 0.7 copy-done
  2.0 0.0 copy-start.1
  2.0 0.7 copy-done.1
  2.7 0.1 shard_map.50
  2.9 19.7 %all_to_all.25 = f32[8,13,4,128]{3,2,1,0:T(4,128)S(1)} all-to-all(f32[8,13,4,128]{3,2,1,0:T(4,128)S(1)} %get-tuple-element.15), channel_id=1, replica_groups={{0,2,4,6,8,10,12,14},{1,3,5,7,9,11,13,15},{16,18,20,22,24,26,28,30},{17..., dimensions={0} | all-to-all | bytes 425984 | tf_op jit(solution)/shard_map/all_to_all | solution.py:252
  22.5 4.5 %all-gather = f32[16,13,4,128]{3,2,1,0:T(4,128)S(1)} all-gather(f32[8,13,4,128]{3,2,1,0:T(4,128)S(1)} %all_to_all.25), channel_id=2, replica_groups={{0,1},{2,3},{4,5},{6,7},{8,9},{10,11},{12,13},{14,15},{16,17},{18,19},{..., dimensions={0}, use_global_device_ids=true | all-gather | bytes 638976 | tf_op jit(solution)/shard_map/all_gather | solution.py:253
  27.0 12.5 %shard_map.51 = (f32[9,512]{1,0:T(8,128)S(1)}, f32[3,512]{1,0:T(4,128)S(1)}, f32[16,3,4,128]{3,2,1,0:T(4,128)S(1)}) custom-call(f32[2,8,13,4,128]{4,3,2,1,0:T(4,128)S(1)} %bitcast.5, f32[9,512]{1,0:T(8,128)S(1)} %get-tuple-element.16.own_ref), custom_call_target="tpu_custom_call" | custom-call | tf_op jit(solution)/shard_map/pallas_call | solution.py:228
  39.6 11.3 %all_to_all.26.gathered_ref.second_ref = f32[16,3,4,128]{3,2,1,0:T(4,128)S(1)} all-to-all(f32[16,3,4,128]{3,2,1,0:T(4,128)S(1)} %get-tuple-element.17), channel_id=1, replica_groups=mesh['tm'=32,'dom'=16] {'dom'}, dimensions={0} | all-to-all | bytes 196608 | tf_op jit(solution)/shard_map/all_to_all | solution.py:261
  50.9 4.3 %shard_map.52 = (f32[3,512]{1,0:T(4,128)S(1)}, f32[3,512]{1,0:T(4,128)S(1)}, f32[16,3,4,128]{3,2,1,0:T(4,128)S(1)}) custom-call(f32[2,8,13,4,128]{4,3,2,1,0:T(4,128)S(1)} %bitcast.6, f32[16,3,4,128]{3,2,1,0:T(4,128)S(1)} %all_to_all.26.gathered_ref.second_ref, f32[9,512]{1,0:T(8,128)S(1)} %get-tuple-element.18.velocity_ref, ...), custom_call_target="tpu_custom_call" | custom-call | tf_op jit(solution)/shard_map/pallas_call | solution.py:228
  55.1 10.9 %all_to_all.27.gathered_ref.third_ref = f32[16,3,4,128]{3,2,1,0:T(4,128)S(1)} all-to-all(f32[16,3,4,128]{3,2,1,0:T(4,128)S(1)} %get-tuple-element.20), channel_id=1, replica_groups=mesh['tm'=32,'dom'=16] {'dom'}, dimensions={0} | all-to-all | bytes 196608 | tf_op jit(solution)/shard_map/all_to_all | solution.py:271
  66.0 4.3 %shard_map.53 = f32[16,3,8,128]{3,2,1,0:T(8,128)S(1)} custom-call(f32[2,8,13,4,128]{4,3,2,1,0:T(4,128)S(1)} %bitcast.7, f32[16,3,4,128]{3,2,1,0:T(4,128)S(1)} %all_to_all.27.gathered_ref.third_ref, f32[9,512]{1,0:T(8,128)S(1)} %get-tuple-element.18.velocity_ref, f32[3,512]{1,0:T(4,128)S(1)} %get-tuple-element.21.swept_ref, ...), custom_call_target="tpu_custom_call" | custom-call | tf_op jit(solution)/shard_map/pallas_call | solution.py:228
  70.4 12.7 %all_to_all.28.quads_ref = f32[16,3,8,128]{3,2,1,0:T(8,128)S(1)} all-to-all(f32[16,3,8,128]{3,2,1,0:T(8,128)S(1)} %shard_map.53), channel_id=1, replica_groups=mesh['tm'=32,'dom'=16] {'dom'}, dimensions={0} | all-to-all | bytes 393216 | tf_op jit(solution)/shard_map/all_to_all | solution.py:282
  83.1 3.0 %shard_map.54 = (f32[15,512]{1,0:T(8,128)S(1)}, f32[32,3,4,128]{3,2,1,0:T(4,128)S(1)}) custom-call(f32[2,8,13,4,128]{4,3,2,1,0:T(4,128)S(1)} %bitcast.8, f32[16,3,4,128]{3,2,1,0:T(4,128)S(1)} %all_to_all.26.gathered_ref.second_ref, f32[16,3,4,128]{3,2,1,0:T(4,128)S(1)} %all_to_all.27.gathered_ref.third_ref, f32[16,3,8,128]{3,2,1,0:T(8,128)S(1)} %all_to_all.28.quads_ref, ...), custom_call_target="tpu_custom_call" | custom-call | tf_op jit(solution)/shard_map/pallas_call | solution.py:228
  86.1 20.5 %all_to_all.29.received_ref = f32[32,3,4,128]{3,2,1,0:T(4,128)S(1)} all-to-all(f32[32,3,4,128]{3,2,1,0:T(4,128)S(1)} %get-tuple-element.24), channel_id=1, replica_groups=mesh['tm'=32,'dom'=16] {'tm'}, dimensions={0} | all-to-all | bytes 393216 | tf_op jit(solution)/shard_map/all_to_all | solution.py:293
  106.6 0.8 shard_map.55
Async XLA Ops:
  0.6 0.7 copy-start.2
  1.3 0.7 copy-start
  2.0 0.7 copy-start.1

commit v3 on v2

--- a/solution.py
+++ b/solution.py
@@ -106,7 +106,27 @@
         store_chunks(ref.at[number], value)
 
 
-def prepare_kernel(nodes_ref, vorticity_ref, coarse_ref, own_ref, mine_ref, send_ref):
+def prepare_kernel(
+    nodes_hbm,
+    vorticity_hbm,
+    coarse_hbm,
+    own_ref,
+    mine_ref,
+    send_ref,
+    nodes_ref,
+    vorticity_ref,
+    coarse_ref,
+    arrived,
+):
+    pairs = [(nodes_hbm, nodes_ref), (vorticity_hbm, vorticity_ref), (coarse_hbm, coarse_ref)]
+    copies = [
+        pltpu.make_async_copy(source, target, arrived.at[number])
+        for number, (source, target) in enumerate(pairs)
+    ]
+    for copy in copies:
+        copy.start()
+    for copy in copies:
+        copy.wait()
     own = nodes_ref[:, 0]
     mine = coarse_ref[...].astype(f32)
     own_ref[...] = own
@@ -170,12 +190,10 @@
             send_ref[number, :, chunks + chunk] = (early + late)[:, lanes]
 
 
-def means_kernel(all_ref, second_ref, third_ref, quads_ref, coarse_ref, means_ref, send_ref, rows):
+def means_kernel(all_ref, second_ref, third_ref, quads_ref, mine_ref, means_ref, send_ref, rows):
     halves, lines = all_ref.shape[:2]
-    width = coarse_ref.shape[1]
-    chunks = width // lane
-    mine = jnp.broadcast_to(coarse_ref[...], (8, width)).T[:, 0:1]
-    total = jnp.zeros((rows.shape[0], width), f32)
+    width = mine_ref.shape[1]
+    coarse = []
     for z in range(lines):
         for h in range(halves):
             number = halves * z + h
@@ -191,12 +209,14 @@
                 0,
             )
             ones = jnp.ones((3, width), f32)
-            rows[...] = jnp.concatenate([*parts_of(values, 3), ones], 0).astype(bf16)
-            theirs = wide(all_ref, h, z, pl.ds(12, 1))
-            same = jnp.where(mine == theirs, 1.0, 0.0).astype(bf16)
-            total = total + lax.dot_general(
-                rows[...], same, (((1,), (1,)), ((), ())), preferred_element_type=f32
-            )
+            lanes = pl.ds(number * width, width)
+            rows[:, lanes] = jnp.concatenate([*parts_of(values, 3), ones], 0).astype(bf16)
+            coarse.append(all_ref[h, z, 12])
+    columns = jnp.concatenate(coarse, 0).T
+    columns = [columns[:, number : number + 1] for number in range(columns.shape[1])]
+    mine = mine_ref[...]
+    same = [jnp.where(column == mine, 1.0, 0.0).astype(bf16) for column in columns]
+    total = jnp.dot(rows[...], jnp.concatenate(same, 0), preferred_element_type=f32)
     means = (total[0:15] + total[15:30] + total[30:45]) / total[45:46]
     means_ref[...] = means
     first_slice = lax.axis_index("tm") == 0
@@ -233,6 +253,24 @@
     )(*operands)
 
 
+def prepare(node_pos, vorticity, coarse_of, copies):
+    width = vorticity.shape[1]
+    nodes = node_pos.reshape(9, 1, width)
+    coarse = coarse_of[None]
+    shapes = [(9, width), (1, width), (copies, 13, width // lane, lane)]
+    return pl.pallas_call(
+        prepare_kernel,
+        out_shape=[jax.ShapeDtypeStruct(shape, f32) for shape in shapes],
+        in_specs=[pl.BlockSpec(memory_space=pltpu.HBM)] * 3,
+        scratch_shapes=[
+            pltpu.VMEM(nodes.shape, f32),
+            pltpu.VMEM(vorticity.shape, f32),
+            pltpu.VMEM(coarse.shape, jnp.int32),
+            pltpu.SemaphoreType.DMA((3,)),
+        ],
+    )(nodes, vorticity, coarse)
+
+
 def body(node_pos, vorticity, coarse_of):
     width = vorticity.shape[1]
     domains = lax.axis_size("dom")
@@ -241,14 +279,7 @@
     chunks = width // lane
     same_core = [[2 * z + h for z in range(lines)] for h in range(2)]
     same_chip = [[2 * z, 2 * z + 1] for z in range(lines)]
-    own, mine, send = call(
-        prepare_kernel,
-        [(9, width), (1, width), (lines, 13, chunks, lane)],
-        [],
-        node_pos.reshape(9, 1, width),
-        vorticity,
-        coarse_of[None],
-    )
+    own, mine, send = prepare(node_pos, vorticity, coarse_of, lines)
     along = lax.all_to_all(send, "dom", 0, 0, axis_index_groups=same_core)
     everyone = lax.all_gather(along, "dom", axis=0, axis_index_groups=same_chip)
     count = domains * width
@@ -283,7 +314,7 @@
     means, send = call(
         means_kernel,
         [(15, width), (slices,) + packed],
-        [(48, width)],
+        [(48, count)],
         everyone,
         seconds,
         thirds,

time: 108 us -> 107 us (level)
  local copies, waits for them, and re-layouts: 2.09 us -> 0.01 us
    unnamed x6 -> x4, local copies, waits for them, and re-layouts: 2.09 us -> 0.01 us
    pallas_call x0 -> x1, Pallas kernels: none -> 1.55 us  [prepare(): pl.pallas_call(prepare_kernel, out_shape=[jax.ShapeDtypeStruct(shape, f32...]
    pallas_call x6 -> x5, Pallas kernels: 25.1 us -> 24.1 us  [call(): pl.pallas_call(kernel, out_shape=[jax.ShapeDtypeStruct(shape, f32) for sh...]
where the time goes in v3:
time: 107 us; the launch traced here: 106 us
  blocking collectives  79.9 us (75%)
  Pallas kernels  25.7 us (24%)
    pallas_call x5, Pallas kernels, call(): pl.pallas_call(kernel, out_shape=[jax.ShapeDtypeStruct(shape, f32) for sh...  24.1 us
    all_to_all x1, blocking collectives, body(): received = lax.all_to_all(send, 'tm', 0, 0)  20.5 us
    all_to_all x1, blocking collectives, body(): along = lax.all_to_all(send, 'dom', 0, 0, axis_index_groups=same_core)  19.9 us
    all_to_all x1, blocking collectives, body(): quads = lax.all_to_all(send, 'dom', 0, 0)  12.7 us
    all_to_all x1, blocking collectives, body(): seconds = lax.all_to_all(send, 'dom', 0, 0)  11.3 us
    all_to_all x1, blocking collectives, body(): thirds = lax.all_to_all(send, 'dom', 0, 0)  10.9 us
    all_gather x1, blocking collectives, body(): everyone = lax.all_gather(along, 'dom', axis=0, axis_index_groups=same_chip)  4.61 us

profile of v3, /device:TPU:1, one launch (start us, length us, event | category | flops | bytes accessed | tf_op | source)
XLA Modules:
  0.0 106.2 jit_solution(6654156153342065493)
XLA Ops:
  0.6 1.6 %shard_map.50 = (f32[9,512]{1,0:T(8,128)}, f32[1,512]{1,0:T(1,128)}, f32[8,13,4,128]{3,2,1,0:T(4,128)}) custom-call(f32[9,1,512]{2,1,0:T(1,128)} %bitcast.9, f32[3,512]{1,0:T(4,128)} %vorticity_hbm.1, s32[1,512]{1,0:T(1,128)} %bitcast.10), custom_call_target="tpu_custom_call" | custom-call | tf_op jit(solution)/shard_map/pallas_call | solution.py:261
  2.2 19.9 %all_to_all.25 = f32[8,13,4,128]{3,2,1,0:T(4,128)S(1)} all-to-all(f32[8,13,4,128]{3,2,1,0:T(4,128)} %get-tuple-element.15), channel_id=1, replica_groups={{0,2,4,6,8,10,12,14},{1,3,5,7,9,11,13,15},{16,18,20,22,24,26,28,30},{17..., dimensions={0} | all-to-all | bytes 425984 | tf_op jit(solution)/shard_map/all_to_all | solution.py:283
  22.1 0.0 copy-start
  22.1 4.6 %all-gather = f32[16,13,4,128]{3,2,1,0:T(4,128)S(1)} all-gather(f32[8,13,4,128]{3,2,1,0:T(4,128)S(1)} %all_to_all.25), channel_id=2, replica_groups={{0,1},{2,3},{4,5},{6,7},{8,9},{10,11},{12,13},{14,15},{16,17},{18,19},{..., dimensions={0}, use_global_device_ids=true | all-gather | bytes 638976 | tf_op jit(solution)/shard_map/all_gather | solution.py:284
  26.7 0.0 copy-done
  26.7 12.5 %shard_map.51 = (f32[9,512]{1,0:T(8,128)S(1)}, f32[3,512]{1,0:T(4,128)S(1)}, f32[16,3,4,128]{3,2,1,0:T(4,128)S(1)}) custom-call(f32[2,8,13,4,128]{4,3,2,1,0:T(4,128)S(1)} %bitcast.5, f32[9,512]{1,0:T(8,128)S(1)} %copy-done), custom_call_target="tpu_custom_call" | custom-call | tf_op jit(solution)/shard_map/pallas_call | solution.py:248
  39.2 11.3 %all_to_all.26.gathered_ref.second_ref = f32[16,3,4,128]{3,2,1,0:T(4,128)S(1)} all-to-all(f32[16,3,4,128]{3,2,1,0:T(4,128)S(1)} %get-tuple-element.17), channel_id=1, replica_groups=mesh['tm'=32,'dom'=16] {'dom'}, dimensions={0} | all-to-all | bytes 196608 | tf_op jit(solution)/shard_map/all_to_all | solution.py:292
  50.5 4.3 %shard_map.52 = (f32[3,512]{1,0:T(4,128)S(1)}, f32[3,512]{1,0:T(4,128)S(1)}, f32[16,3,4,128]{3,2,1,0:T(4,128)S(1)}) custom-call(f32[2,8,13,4,128]{4,3,2,1,0:T(4,128)S(1)} %bitcast.6, f32[16,3,4,128]{3,2,1,0:T(4,128)S(1)} %all_to_all.26.gathered_ref.second_ref, f32[9,512]{1,0:T(8,128)S(1)} %get-tuple-element.18.velocity_ref, ...), custom_call_target="tpu_custom_call" | custom-call | tf_op jit(solution)/shard_map/pallas_call | solution.py:248
  54.8 10.9 %all_to_all.27.gathered_ref.third_ref = f32[16,3,4,128]{3,2,1,0:T(4,128)S(1)} all-to-all(f32[16,3,4,128]{3,2,1,0:T(4,128)S(1)} %get-tuple-element.20), channel_id=1, replica_groups=mesh['tm'=32,'dom'=16] {'dom'}, dimensions={0} | all-to-all | bytes 196608 | tf_op jit(solution)/shard_map/all_to_all | solution.py:302
  65.7 4.3 %shard_map.53 = f32[16,3,8,128]{3,2,1,0:T(8,128)S(1)} custom-call(f32[2,8,13,4,128]{4,3,2,1,0:T(4,128)S(1)} %bitcast.7, f32[16,3,4,128]{3,2,1,0:T(4,128)S(1)} %all_to_all.27.gathered_ref.third_ref, f32[9,512]{1,0:T(8,128)S(1)} %get-tuple-element.18.velocity_ref, f32[3,512]{1,0:T(4,128)S(1)} %get-tuple-element.21.swept_ref, ...), custom_call_target="tpu_custom_call" | custom-call | tf_op jit(solution)/shard_map/pallas_call | solution.py:248
  70.0 0.0 copy-start.1
  70.1 12.7 %all_to_all.28.quads_ref = f32[16,3,8,128]{3,2,1,0:T(8,128)S(1)} all-to-all(f32[16,3,8,128]{3,2,1,0:T(8,128)S(1)} %shard_map.53), channel_id=1, replica_groups=mesh['tm'=32,'dom'=16] {'dom'}, dimensions={0} | all-to-all | bytes 393216 | tf_op jit(solution)/shard_map/all_to_all | solution.py:313
  82.7 0.0 copy-done.1
  82.7 2.2 %shard_map.54 = (f32[15,512]{1,0:T(8,128)S(1)}, f32[32,3,4,128]{3,2,1,0:T(4,128)S(1)}) custom-call(f32[2,8,13,4,128]{4,3,2,1,0:T(4,128)S(1)} %bitcast.8, f32[16,3,4,128]{3,2,1,0:T(4,128)S(1)} %all_to_all.26.gathered_ref.second_ref, f32[16,3,4,128]{3,2,1,0:T(4,128)S(1)} %all_to_all.27.gathered_ref.third_ref, f32[16,3,8,128]{3,2,1,0:T(8,128)S(1)} %all_to_all.28.quads_ref, ...), custom_call_target="tpu_custom_call" | custom-call | tf_op jit(solution)/shard_map/pallas_call | solution.py:248
  85.0 20.5 %all_to_all.29.received_ref = f32[32,3,4,128]{3,2,1,0:T(4,128)S(1)} all-to-all(f32[32,3,4,128]{3,2,1,0:T(4,128)S(1)} %get-tuple-element.24), channel_id=1, replica_groups=mesh['tm'=32,'dom'=16] {'tm'}, dimensions={0} | all-to-all | bytes 393216 | tf_op jit(solution)/shard_map/all_to_all | solution.py:324
  105.5 0.8 shard_map.55
Async XLA Ops:
  22.1 4.6 %copy-start = (f32[9,512]{1,0:T(8,128)S(1)}, f32[9,512]{1,0:T(8,128)}, u32[]{:S(2)}) copy-start(f32[9,512]{1,0:T(8,128)} %get-tuple-element.16.own_ref) | copy-start | bytes 55300
  70.0 12.7 %copy-start.1 = (f32[1,512]{1,0:T(1,128)S(1)}, f32[1,512]{1,0:T(1,128)}, u32[]{:S(2)}) copy-start(f32[1,512]{1,0:T(1,128)} %get-tuple-element.23.mine_ref) | copy-start | bytes 6148

commit v4 on v3

--- a/solution.py
+++ b/solution.py
@@ -268,7 +268,8 @@
             pltpu.VMEM(coarse.shape, jnp.int32),
             pltpu.SemaphoreType.DMA((3,)),
         ],
-    )(nodes, vorticity, coarse)
+        compiler_params=pltpu.CompilerParams(vmem_limit_bytes=vmem_bytes),
+    )(*[pltpu.with_memory_space_constraint(x, pltpu.HBM) for x in (nodes, vorticity, coarse)])
 
 
 def body(node_pos, vorticity, coarse_of):

time: 107 us -> 106 us (level)
  no operation moved by 1% of the time
where the time goes in v4:
time: 106 us; the launch traced here: 105 us
  blocking collectives  79.5 us (75%)
  Pallas kernels  25 us (24%)
    pallas_call x5, Pallas kernels, call(): pl.pallas_call(kernel, out_shape=[jax.ShapeDtypeStruct(shape, f32) for sh...  24.1 us
    all_to_all x1, blocking collectives, body(): received = lax.all_to_all(send, 'tm', 0, 0)  20.5 us
    all_to_all x1, blocking collectives, body(): along = lax.all_to_all(send, 'dom', 0, 0, axis_index_groups=same_core)  19.7 us
    all_to_all x1, blocking collectives, body(): quads = lax.all_to_all(send, 'dom', 0, 0)  12.7 us
    all_to_all x1, blocking collectives, body(): seconds = lax.all_to_all(send, 'dom', 0, 0)  11.3 us
    all_to_all x1, blocking collectives, body(): thirds = lax.all_to_all(send, 'dom', 0, 0)  10.9 us
    all_gather x1, blocking collectives, body(): everyone = lax.all_gather(along, 'dom', axis=0, axis_index_groups=same_chip)  4.48 us

profile of v4, /device:TPU:1, one launch (start us, length us, event | category | flops | bytes accessed | tf_op | source)
XLA Modules:
  0.0 105.2 jit_solution(5361151763083272879)
XLA Ops:
  0.6 0.9 shard_map.50
  1.5 19.7 %all_to_all.25 = f32[8,13,4,128]{3,2,1,0:T(4,128)S(1)} all-to-all(f32[8,13,4,128]{3,2,1,0:T(4,128)S(1)} %get-tuple-element.15), channel_id=1, replica_groups={{0,2,4,6,8,10,12,14},{1,3,5,7,9,11,13,15},{16,18,20,22,24,26,28,30},{17..., dimensions={0} | all-to-all | bytes 425984 | tf_op jit(solution)/shard_map/all_to_all | solution.py:284
  21.2 4.5 %all-gather = f32[16,13,4,128]{3,2,1,0:T(4,128)S(1)} all-gather(f32[8,13,4,128]{3,2,1,0:T(4,128)S(1)} %all_to_all.25), channel_id=2, replica_groups={{0,1},{2,3},{4,5},{6,7},{8,9},{10,11},{12,13},{14,15},{16,17},{18,19},{..., dimensions={0}, use_global_device_ids=true | all-gather | bytes 638976 | tf_op jit(solution)/shard_map/all_gather | solution.py:285
  25.7 12.5 %shard_map.51 = (f32[9,512]{1,0:T(8,128)S(1)}, f32[3,512]{1,0:T(4,128)S(1)}, f32[16,3,4,128]{3,2,1,0:T(4,128)S(1)}) custom-call(f32[2,8,13,4,128]{4,3,2,1,0:T(4,128)S(1)} %bitcast.5, f32[9,512]{1,0:T(8,128)S(1)} %get-tuple-element.16.own_ref), custom_call_target="tpu_custom_call" | custom-call | tf_op jit(solution)/shard_map/pallas_call | solution.py:248
  38.2 11.3 %all_to_all.26.gathered_ref.second_ref = f32[16,3,4,128]{3,2,1,0:T(4,128)S(1)} all-to-all(f32[16,3,4,128]{3,2,1,0:T(4,128)S(1)} %get-tuple-element.17), channel_id=1, replica_groups=mesh['tm'=32,'dom'=16] {'dom'}, dimensions={0} | all-to-all | bytes 196608 | tf_op jit(solution)/shard_map/all_to_all | solution.py:293
  49.5 4.3 %shard_map.52 = (f32[3,512]{1,0:T(4,128)S(1)}, f32[3,512]{1,0:T(4,128)S(1)}, f32[16,3,4,128]{3,2,1,0:T(4,128)S(1)}) custom-call(f32[2,8,13,4,128]{4,3,2,1,0:T(4,128)S(1)} %bitcast.6, f32[16,3,4,128]{3,2,1,0:T(4,128)S(1)} %all_to_all.26.gathered_ref.second_ref, f32[9,512]{1,0:T(8,128)S(1)} %get-tuple-element.18.velocity_ref, ...), custom_call_target="tpu_custom_call" | custom-call | tf_op jit(solution)/shard_map/pallas_call | solution.py:248
  53.8 10.9 %all_to_all.27.gathered_ref.third_ref = f32[16,3,4,128]{3,2,1,0:T(4,128)S(1)} all-to-all(f32[16,3,4,128]{3,2,1,0:T(4,128)S(1)} %get-tuple-element.20), channel_id=1, replica_groups=mesh['tm'=32,'dom'=16] {'dom'}, dimensions={0} | all-to-all | bytes 196608 | tf_op jit(solution)/shard_map/all_to_all | solution.py:303
  64.7 4.3 %shard_map.53 = f32[16,3,8,128]{3,2,1,0:T(8,128)S(1)} custom-call(f32[2,8,13,4,128]{4,3,2,1,0:T(4,128)S(1)} %bitcast.7, f32[16,3,4,128]{3,2,1,0:T(4,128)S(1)} %all_to_all.27.gathered_ref.third_ref, f32[9,512]{1,0:T(8,128)S(1)} %get-tuple-element.18.velocity_ref, f32[3,512]{1,0:T(4,128)S(1)} %get-tuple-element.21.swept_ref, ...), custom_call_target="tpu_custom_call" | custom-call | tf_op jit(solution)/shard_map/pallas_call | solution.py:248
  69.0 12.7 %all_to_all.28.quads_ref = f32[16,3,8,128]{3,2,1,0:T(8,128)S(1)} all-to-all(f32[16,3,8,128]{3,2,1,0:T(8,128)S(1)} %shard_map.53), channel_id=1, replica_groups=mesh['tm'=32,'dom'=16] {'dom'}, dimensions={0} | all-to-all | bytes 393216 | tf_op jit(solution)/shard_map/all_to_all | solution.py:314
  81.7 2.2 %shard_map.54 = (f32[15,512]{1,0:T(8,128)S(1)}, f32[32,3,4,128]{3,2,1,0:T(4,128)S(1)}) custom-call(f32[2,8,13,4,128]{4,3,2,1,0:T(4,128)S(1)} %bitcast.8, f32[16,3,4,128]{3,2,1,0:T(4,128)S(1)} %all_to_all.26.gathered_ref.second_ref, f32[16,3,4,128]{3,2,1,0:T(4,128)S(1)} %all_to_all.27.gathered_ref.third_ref, f32[16,3,8,128]{3,2,1,0:T(8,128)S(1)} %all_to_all.28.quads_ref, ...), custom_call_target="tpu_custom_call" | custom-call | tf_op jit(solution)/shard_map/pallas_call | solution.py:248
  83.9 20.5 %all_to_all.29.received_ref = f32[32,3,4,128]{3,2,1,0:T(4,128)S(1)} all-to-all(f32[32,3,4,128]{3,2,1,0:T(4,128)S(1)} %get-tuple-element.24), channel_id=1, replica_groups=mesh['tm'=32,'dom'=16] {'tm'}, dimensions={0} | all-to-all | bytes 393216 | tf_op jit(solution)/shard_map/all_to_all | solution.py:325
  104.4 0.8 shard_map.55

commit v5 on v4

--- a/solution.py
+++ b/solution.py
@@ -14,8 +14,8 @@
 dt_slice = 0.5
 node_weights = ((5.0 / 24.0, 1.0 / 3.0, -1.0 / 24.0), (-1.0 / 24.0, 1.0 / 3.0, 5.0 / 24.0))
 vmem_bytes = 52 << 20
-source_rows = 18
-moment_rows = 16
+part_blocks = 2
+rows_cycle = 8
 
 
 def high_part(value):
@@ -47,42 +47,65 @@
     )
 
 
-def source_features(p):
+def cyclic(rows):
+    return jnp.concatenate([rows, rows, rows[0:2]], 0)
+
+
+def rotated(rows, number):
+    return pltpu.roll(rows, rows_cycle - number, 0)
+
+
+def source_rows(p, w, leading):
+    w = w * inv_four_pi
     high, low = parts_of(p, 2)
-    sq = parts_of(norm_sq(high + low), 3)
-    one = jnp.ones_like(sq[0])
-    return jnp.concatenate([high, high, low, low, *sq, one, one, one], 0).astype(bf16)
-
-
-def target_features(x):
+    near = jnp.where(leading, high, low)
+    summed = high + low
+    first, second, third = parts_of(summed * summed, 3)
+    norms = jnp.where(leading, first, second)
+    last = jnp.where(leading, third, 1.0)
+    features = jnp.concatenate([near, near, norms, last], 0).astype(bf16)
+    high, low = parts_of(w, 2)
+    strengths = jnp.where(leading, high, low)
+    products = jnp.where(leading, rotated(w, 1), rotated(w, 2)) * jnp.where(
+        leading, rotated(p, 2), rotated(p, 1)
+    )
+    crossed = products - jnp.where(leading, rotated(products, 3), rotated(products, 5))
+    high, low = parts_of(crossed, 2)
+    moments = jnp.concatenate([strengths, jnp.where(leading, high, low)], 0).astype(bf16)
+    return features, moments
+
+
+def target_rows(x):
     high, low = parts_of(x, 2)
-    sq = parts_of(norm_sq(high + low) + sigma_sq, 3)
-    one = jnp.ones_like(sq[0])
-    rows = [-2.0 * high, -2.0 * low, -2.0 * high, -2.0 * low, one, one, one, *sq]
+    norms = parts_of(norm_sq(high + low) + sigma_sq, 3)
+    none = jnp.zeros((2, x.shape[1]), f32)
+    one = jnp.ones_like(x)
+    high, low = -2.0 * high, -2.0 * low
+    rows = [high, high, none, low, low, none, one, one, none, one, *norms, none]
     return jnp.concatenate(rows, 0).astype(bf16)
 
 
-def source_moments(p, w):
-    w = w * inv_four_pi
-    pad = jnp.zeros((moment_rows - 12, p.shape[1]), f32)
-    return jnp.concatenate([*parts_of(w, 2), *parts_of(cross(w, p), 2), pad], 0).astype(bf16)
-
-
-def field(blocks, x, center, features, moments):
+def field(blocks, x, center):
     width = x.shape[1]
-    for number, (p, w) in enumerate(blocks):
-        lanes = pl.ds(number * width, width)
-        shifted = p - center
-        features[:, lanes] = source_features(shifted)
-        moments[:, lanes] = source_moments(shifted, w)
+    leading = lax.broadcasted_iota(jnp.int32, (rows_cycle, width), 0) < 3
+    centers = cyclic(jnp.broadcast_to(center, x.shape))
     x = x - center
-    sq = lax.dot_general(
-        features[...], target_features(x), (((0,), (0,)), ((), ())), preferred_element_type=f32
-    )
-    root = lax.rsqrt(sq)
-    kernel = (root * root * root).astype(bf16)
-    summed = jnp.dot(moments[...], kernel, preferred_element_type=f32)
-    return cross(summed[0:3] + summed[3:6], x) - (summed[6:9] + summed[9:12])
+    targets = target_rows(x)
+    total = jnp.zeros((2 * rows_cycle, width), f32)
+    for begin in range(0, len(blocks), part_blocks):
+        rows = [
+            source_rows(cyclic(p) - centers, cyclic(w), leading)
+            for p, w in blocks[begin : begin + part_blocks]
+        ]
+        features = jnp.concatenate([pair[0] for pair in rows], 1)
+        moments = jnp.concatenate([pair[1] for pair in rows], 1)
+        sq = lax.dot_general(
+            features, targets, (((0,), (0,)), ((), ())), preferred_element_type=f32
+        )
+        root = lax.rsqrt(sq)
+        kernel = (root * root * root).astype(bf16)
+        total = total + jnp.dot(moments, kernel, preferred_element_type=f32)
+    return cross(total[0:3] + total[3:6], x) - (total[8:11] - total[11:14])
 
 
 def quad(row, a, b, c):
@@ -134,7 +157,7 @@
     spread_out(send_ref, jnp.concatenate([own, vorticity_ref[...], mine], 0))
 
 
-def nodes_kernel(all_ref, own_ref, velocity_ref, second_ref, send_ref, features, moments):
+def nodes_kernel(all_ref, own_ref, velocity_ref, second_ref, send_ref):
     halves, lines = all_ref.shape[:2]
     center = own_ref[0:3, 0:1]
     found = []
@@ -145,7 +168,7 @@
             for z in range(lines)
             for h in range(halves)
         ]
-        found.append(field(blocks, own_ref[rows], center, features, moments))
+        found.append(field(blocks, own_ref[rows], center))
     velocity_ref[...] = jnp.concatenate(found, 0)
     second = own_ref[0:3] + quad(node_weights[0], *found)
     second_ref[...] = second
@@ -162,11 +185,11 @@
 
 
 def second_kernel(
-    all_ref, gathered_ref, velocity_ref, second_ref, swept_ref, third_ref, send_ref, features, moments
+    all_ref, gathered_ref, velocity_ref, second_ref, swept_ref, third_ref, send_ref
 ):
     second = second_ref[...]
     blocks = swept_blocks(all_ref, gathered_ref)
-    swept = field(blocks, second, second[:, 0:1], features, moments)
+    swept = field(blocks, second, second[:, 0:1])
     swept_ref[...] = swept
     nodes = [velocity_ref[pl.ds(3 * node, 3)] for node in range(3)]
     third = second + 0.5 * dt_slice * (swept - nodes[1]) + quad(node_weights[1], *nodes)
@@ -175,11 +198,11 @@
 
 
 def third_kernel(
-    all_ref, gathered_ref, velocity_ref, swept_ref, third_ref, send_ref, features, moments
+    all_ref, gathered_ref, velocity_ref, swept_ref, third_ref, send_ref
 ):
     third = third_ref[...]
     blocks = swept_blocks(all_ref, gathered_ref)
-    last = field(blocks, third, third[:, 0:1], features, moments)
+    last = field(blocks, third, third[:, 0:1])
     early = quad(node_weights[0], velocity_ref[0:3], swept_ref[...], last)
     late = quad(node_weights[1], velocity_ref[0:3], swept_ref[...], last)
     chunks = early.shape[1] // lane
@@ -190,10 +213,11 @@
             send_ref[number, :, chunks + chunk] = (early + late)[:, lanes]
 
 
-def means_kernel(all_ref, second_ref, third_ref, quads_ref, mine_ref, means_ref, send_ref, rows):
+def means_kernel(all_ref, second_ref, third_ref, quads_ref, mine_ref, means_ref, send_ref):
     halves, lines = all_ref.shape[:2]
     width = mine_ref.shape[1]
-    coarse = []
+    ones = jnp.ones((3, width), f32)
+    rows, coarse = [], []
     for z in range(lines):
         for h in range(halves):
             number = halves * z + h
@@ -208,15 +232,23 @@
                 ],
                 0,
             )
-            ones = jnp.ones((3, width), f32)
-            lanes = pl.ds(number * width, width)
-            rows[:, lanes] = jnp.concatenate([*parts_of(values, 3), ones], 0).astype(bf16)
+            rows.append(jnp.concatenate([*parts_of(values, 3), ones], 0).astype(bf16))
             coarse.append(all_ref[h, z, 12])
     columns = jnp.concatenate(coarse, 0).T
-    columns = [columns[:, number : number + 1] for number in range(columns.shape[1])]
     mine = mine_ref[...]
-    same = [jnp.where(column == mine, 1.0, 0.0).astype(bf16) for column in columns]
-    total = jnp.dot(rows[...], jnp.concatenate(same, 0), preferred_element_type=f32)
+    total = jnp.zeros((48, width), f32)
+    for begin in range(0, len(rows), 2 * part_blocks):
+        end = begin + 2 * part_blocks
+        chunks = range(begin * width // lane, end * width // lane)
+        same = [
+            jnp.where(columns[:, chunk : chunk + 1] == mine, 1.0, 0.0).astype(bf16)
+            for chunk in chunks
+        ]
+        total = total + jnp.dot(
+            jnp.concatenate(rows[begin:end], 1),
+            jnp.concatenate(same, 0),
+            preferred_element_type=f32,
+        )
     means = (total[0:15] + total[15:30] + total[30:45]) / total[45:46]
     means_ref[...] = means
     first_slice = lax.axis_index("tm") == 0
@@ -244,11 +276,10 @@
     end_ref[:, 0] = picked[0:3] + picked[3:6] + picked[6:9]
 
 
-def call(kernel, shapes, scratch, *operands):
+def call(kernel, shapes, *operands):
     return pl.pallas_call(
         kernel,
         out_shape=[jax.ShapeDtypeStruct(shape, f32) for shape in shapes],
-        scratch_shapes=[pltpu.VMEM(shape, bf16) for shape in scratch],
         compiler_params=pltpu.CompilerParams(vmem_limit_bytes=vmem_bytes),
     )(*operands)
 
@@ -283,18 +314,15 @@
     own, mine, send = prepare(node_pos, vorticity, coarse_of, lines)
     along = lax.all_to_all(send, "dom", 0, 0, axis_index_groups=same_core)
     everyone = lax.all_gather(along, "dom", axis=0, axis_index_groups=same_chip)
-    count = domains * width
-    scratch = [(source_rows, count), (moment_rows, count)]
     three = (3, width)
     packed = (3, chunks, lane)
     velocity, second, send = call(
-        nodes_kernel, [(9, width), three, (domains,) + packed], scratch, everyone, own
+        nodes_kernel, [(9, width), three, (domains,) + packed], everyone, own
     )
     seconds = lax.all_to_all(send, "dom", 0, 0)
     swept, third, send = call(
         second_kernel,
         [three, three, (domains,) + packed],
-        scratch,
         everyone,
         seconds,
         velocity,
@@ -304,7 +332,6 @@
     (send,) = call(
         third_kernel,
         [(domains, 3, 2 * chunks, lane)],
-        scratch,
         everyone,
         thirds,
         velocity,
@@ -315,7 +342,6 @@
     means, send = call(
         means_kernel,
         [(15, width), (slices,) + packed],
-        [(48, count)],
         everyone,
         seconds,
         thirds,
@@ -326,7 +352,6 @@
     fine_nodes, coarse_end = call(
         ends_kernel,
         [(9, 1, width), (3, 1, width // 2)],
-        [],
         received,
         means,
         own,

time: 106 us -> 104 us (0.981)
  Pallas kernels: 25 us -> 22.9 us
    pallas_call x5, Pallas kernels: 24.1 us -> 22.1 us  [call(): pl.pallas_call(kernel, out_shape=[jax.ShapeDtypeStruct(shape, f32) for sh...]
where the time goes in v5:
time: 104 us; the launch traced here: 103 us
  blocking collectives  79.5 us (76%)
  Pallas kernels  22.9 us (22%)
    pallas_call x5, Pallas kernels, call(): pl.pallas_call(kernel, out_shape=[jax.ShapeDtypeStruct(shape, f32) for sh...  22.1 us
    all_to_all x1, blocking collectives, body(): received = lax.all_to_all(send, 'tm', 0, 0)  20.5 us
    all_to_all x1, blocking collectives, body(): along = lax.all_to_all(send, 'dom', 0, 0, axis_index_groups=same_core)  19.7 us
    all_to_all x1, blocking collectives, body(): quads = lax.all_to_all(send, 'dom', 0, 0)  12.7 us
    all_to_all x1, blocking collectives, body(): seconds = lax.all_to_all(send, 'dom', 0, 0)  11.3 us
    all_to_all x1, blocking collectives, body(): thirds = lax.all_to_all(send, 'dom', 0, 0)  10.9 us
    all_gather x1, blocking collectives, body(): everyone = lax.all_gather(along, 'dom', axis=0, axis_index_groups=same_chip)  4.48 us

profile of v5, /device:TPU:1, one launch (start us, length us, event | category | flops | bytes accessed | tf_op | source)
XLA Modules:
  0.0 103.2 jit_solution(15089803421399605783)
XLA Ops:
  0.6 0.9 shard_map.50
  1.5 19.7 %all_to_all.25 = f32[8,13,4,128]{3,2,1,0:T(4,128)S(1)} all-to-all(f32[8,13,4,128]{3,2,1,0:T(4,128)S(1)} %get-tuple-element.15), channel_id=1, replica_groups={{0,2,4,6,8,10,12,14},{1,3,5,7,9,11,13,15},{16,18,20,22,24,26,28,30},{17..., dimensions={0} | all-to-all | bytes 425984 | tf_op jit(solution)/shard_map/all_to_all | solution.py:315
  21.2 4.5 %all-gather = f32[16,13,4,128]{3,2,1,0:T(4,128)S(1)} all-gather(f32[8,13,4,128]{3,2,1,0:T(4,128)S(1)} %all_to_all.25), channel_id=2, replica_groups={{0,1},{2,3},{4,5},{6,7},{8,9},{10,11},{12,13},{14,15},{16,17},{18,19},{..., dimensions={0}, use_global_device_ids=true | all-gather | bytes 638976 | tf_op jit(solution)/shard_map/all_gather | solution.py:316
  25.7 11.0 %shard_map.51 = (f32[9,512]{1,0:T(8,128)S(1)}, f32[3,512]{1,0:T(4,128)S(1)}, f32[16,3,4,128]{3,2,1,0:T(4,128)S(1)}) custom-call(f32[2,8,13,4,128]{4,3,2,1,0:T(4,128)S(1)} %bitcast.5, f32[9,512]{1,0:T(8,128)S(1)} %get-tuple-element.16.own_ref), custom_call_target="tpu_custom_call" | custom-call | tf_op jit(solution)/shard_map/pallas_call | solution.py:280
  36.7 11.3 %all_to_all.26.gathered_ref.second_ref = f32[16,3,4,128]{3,2,1,0:T(4,128)S(1)} all-to-all(f32[16,3,4,128]{3,2,1,0:T(4,128)S(1)} %get-tuple-element.17), channel_id=1, replica_groups=mesh['tm'=32,'dom'=16] {'dom'}, dimensions={0} | all-to-all | bytes 196608 | tf_op jit(solution)/shard_map/all_to_all | solution.py:322
  48.1 3.9 %shard_map.52 = (f32[3,512]{1,0:T(4,128)S(1)}, f32[3,512]{1,0:T(4,128)S(1)}, f32[16,3,4,128]{3,2,1,0:T(4,128)S(1)}) custom-call(f32[2,8,13,4,128]{4,3,2,1,0:T(4,128)S(1)} %bitcast.6, f32[16,3,4,128]{3,2,1,0:T(4,128)S(1)} %all_to_all.26.gathered_ref.second_ref, f32[9,512]{1,0:T(8,128)S(1)} %get-tuple-element.18.velocity_ref, ...), custom_call_target="tpu_custom_call" | custom-call | tf_op jit(solution)/shard_map/pallas_call | solution.py:280
  52.0 10.9 %all_to_all.27.gathered_ref.third_ref = f32[16,3,4,128]{3,2,1,0:T(4,128)S(1)} all-to-all(f32[16,3,4,128]{3,2,1,0:T(4,128)S(1)} %get-tuple-element.20), channel_id=1, replica_groups=mesh['tm'=32,'dom'=16] {'dom'}, dimensions={0} | all-to-all | bytes 196608 | tf_op jit(solution)/shard_map/all_to_all | solution.py:331
  62.8 4.0 %shard_map.53 = f32[16,3,8,128]{3,2,1,0:T(8,128)S(1)} custom-call(f32[2,8,13,4,128]{4,3,2,1,0:T(4,128)S(1)} %bitcast.7, f32[16,3,4,128]{3,2,1,0:T(4,128)S(1)} %all_to_all.27.gathered_ref.third_ref, f32[9,512]{1,0:T(8,128)S(1)} %get-tuple-element.18.velocity_ref, f32[3,512]{1,0:T(4,128)S(1)} %get-tuple-element.21.swept_ref, ...), custom_call_target="tpu_custom_call" | custom-call | tf_op jit(solution)/shard_map/pallas_call | solution.py:280
  66.8 12.7 %all_to_all.28.quads_ref = f32[16,3,8,128]{3,2,1,0:T(8,128)S(1)} all-to-all(f32[16,3,8,128]{3,2,1,0:T(8,128)S(1)} %shard_map.53), channel_id=1, replica_groups=mesh['tm'=32,'dom'=16] {'dom'}, dimensions={0} | all-to-all | bytes 393216 | tf_op jit(solution)/shard_map/all_to_all | solution.py:341
  79.5 2.4 %shard_map.54 = (f32[15,512]{1,0:T(8,128)S(1)}, f32[32,3,4,128]{3,2,1,0:T(4,128)S(1)}) custom-call(f32[2,8,13,4,128]{4,3,2,1,0:T(4,128)S(1)} %bitcast.8, f32[16,3,4,128]{3,2,1,0:T(4,128)S(1)} %all_to_all.26.gathered_ref.second_ref, f32[16,3,4,128]{3,2,1,0:T(4,128)S(1)} %all_to_all.27.gathered_ref.third_ref, f32[16,3,8,128]{3,2,1,0:T(8,128)S(1)} %all_to_all.28.quads_ref, ...), custom_call_target="tpu_custom_call" | custom-call | tf_op jit(solution)/shard_map/pallas_call | solution.py:280
  81.9 20.5 %all_to_all.29.received_ref = f32[32,3,4,128]{3,2,1,0:T(4,128)S(1)} all-to-all(f32[32,3,4,128]{3,2,1,0:T(4,128)S(1)} %get-tuple-element.24), channel_id=1, replica_groups=mesh['tm'=32,'dom'=16] {'tm'}, dimensions={0} | all-to-all | bytes 393216 | tf_op jit(solution)/shard_map/all_to_all | solution.py:351
  102.4 0.8 shard_map.55

commit v6 on v5

--- a/solution.py
+++ b/solution.py
@@ -85,8 +85,9 @@
     return jnp.concatenate(rows, 0).astype(bf16)
 
 
-def field(blocks, x, center):
+def field(blocks, x):
     width = x.shape[1]
+    center = jnp.mean(x, axis=1, keepdims=True)
     leading = lax.broadcasted_iota(jnp.int32, (rows_cycle, width), 0) < 3
     centers = cyclic(jnp.broadcast_to(center, x.shape))
     x = x - center
@@ -159,7 +160,6 @@
 
 def nodes_kernel(all_ref, own_ref, velocity_ref, second_ref, send_ref):
     halves, lines = all_ref.shape[:2]
-    center = own_ref[0:3, 0:1]
     found = []
     for node in range(3):
         rows = pl.ds(3 * node, 3)
@@ -168,7 +168,7 @@
             for z in range(lines)
             for h in range(halves)
         ]
-        found.append(field(blocks, own_ref[rows], center))
+        found.append(field(blocks, own_ref[rows]))
     velocity_ref[...] = jnp.concatenate(found, 0)
     second = own_ref[0:3] + quad(node_weights[0], *found)
     second_ref[...] = second
@@ -189,7 +189,7 @@
 ):
     second = second_ref[...]
     blocks = swept_blocks(all_ref, gathered_ref)
-    swept = field(blocks, second, second[:, 0:1])
+    swept = field(blocks, second)
     swept_ref[...] = swept
     nodes = [velocity_ref[pl.ds(3 * node, 3)] for node in range(3)]
     third = second + 0.5 * dt_slice * (swept - nodes[1]) + quad(node_weights[1], *nodes)
@@ -202,7 +202,7 @@
 ):
     third = third_ref[...]
     blocks = swept_blocks(all_ref, gathered_ref)
-    last = field(blocks, third, third[:, 0:1])
+    last = field(blocks, third)
     early = quad(node_weights[0], velocity_ref[0:3], swept_ref[...], last)
     late = quad(node_weights[1], velocity_ref[0:3], swept_ref[...], last)
     chunks = early.shape[1] // lane
@@ -216,7 +216,7 @@
 def means_kernel(all_ref, second_ref, third_ref, quads_ref, mine_ref, means_ref, send_ref):
     halves, lines = all_ref.shape[:2]
     width = mine_ref.shape[1]
-    ones = jnp.ones((3, width), f32)
+    ones = jnp.ones((1, width), f32)
     rows, coarse = [], []
     for z in range(lines):
         for h in range(halves):
@@ -229,16 +229,17 @@
                     wide(third_ref, number, pl.ds(0, 3)),
                     both[:, :width],
                     both[:, width:],
+                    ones,
                 ],
                 0,
             )
-            rows.append(jnp.concatenate([*parts_of(values, 3), ones], 0).astype(bf16))
+            rows.append(jnp.concatenate(parts_of(values, 2), 0).astype(bf16))
             coarse.append(all_ref[h, z, 12])
     columns = jnp.concatenate(coarse, 0).T
     mine = mine_ref[...]
-    total = jnp.zeros((48, width), f32)
-    for begin in range(0, len(rows), 2 * part_blocks):
-        end = begin + 2 * part_blocks
+    total = jnp.zeros((32, width), f32)
+    for begin in range(0, len(rows), part_blocks):
+        end = begin + part_blocks
         chunks = range(begin * width // lane, end * width // lane)
         same = [
             jnp.where(columns[:, chunk : chunk + 1] == mine, 1.0, 0.0).astype(bf16)
@@ -249,7 +250,8 @@
             jnp.concatenate(same, 0),
             preferred_element_type=f32,
         )
-    means = (total[0:15] + total[15:30] + total[30:45]) / total[45:46]
+    total = total[0:16] + total[16:32]
+    means = total[0:15] / total[15:16]
     means_ref[...] = means
     first_slice = lax.axis_index("tm") == 0
     spread_out(send_ref, means[12:15] + jnp.where(first_slice, means[0:3], 0.0))

time: 104 us -> 103 us (level)
  no operation moved by 1% of the time
where the time goes in v6:
time: 103 us
  blocking collectives  79.5 us (77%)
  Pallas kernels  22.8 us (22%)
    pallas_call x5, Pallas kernels, call(): pl.pallas_call(kernel, out_shape=[jax.ShapeDtypeStruct(shape, f32) for sh...  21.9 us
    all_to_all x1, blocking collectives, body(): received = lax.all_to_all(send, 'tm', 0, 0)  20.5 us
    all_to_all x1, blocking collectives, body(): along = lax.all_to_all(send, 'dom', 0, 0, axis_index_groups=same_core)  19.7 us
    all_to_all x1, blocking collectives, body(): quads = lax.all_to_all(send, 'dom', 0, 0)  12.7 us
    all_to_all x1, blocking collectives, body(): seconds = lax.all_to_all(send, 'dom', 0, 0)  11.3 us
    all_to_all x1, blocking collectives, body(): thirds = lax.all_to_all(send, 'dom', 0, 0)  10.9 us
    all_gather x1, blocking collectives, body(): everyone = lax.all_gather(along, 'dom', axis=0, axis_index_groups=same_chip)  4.48 us

profile of v6, /device:TPU:1, one launch (start us, length us, event | category | flops | bytes accessed | tf_op | source)
XLA Modules:
  0.0 102.9 jit_solution(16266829781644331514)
XLA Ops:
  0.6 0.9 shard_map.50
  1.5 19.7 %all_to_all.25 = f32[8,13,4,128]{3,2,1,0:T(4,128)S(1)} all-to-all(f32[8,13,4,128]{3,2,1,0:T(4,128)S(1)} %get-tuple-element.15), channel_id=1, replica_groups={{0,2,4,6,8,10,12,14},{1,3,5,7,9,11,13,15},{16,18,20,22,24,26,28,30},{17..., dimensions={0} | all-to-all | bytes 425984 | tf_op jit(solution)/shard_map/all_to_all | solution.py:317
  21.2 4.5 %all-gather = f32[16,13,4,128]{3,2,1,0:T(4,128)S(1)} all-gather(f32[8,13,4,128]{3,2,1,0:T(4,128)S(1)} %all_to_all.25), channel_id=2, replica_groups={{0,1},{2,3},{4,5},{6,7},{8,9},{10,11},{12,13},{14,15},{16,17},{18,19},{..., dimensions={0}, use_global_device_ids=true | all-gather | bytes 638976 | tf_op jit(solution)/shard_map/all_gather | solution.py:318
  25.7 11.2 %shard_map.51 = (f32[9,512]{1,0:T(8,128)S(1)}, f32[3,512]{1,0:T(4,128)S(1)}, f32[16,3,4,128]{3,2,1,0:T(4,128)S(1)}) custom-call(f32[2,8,13,4,128]{4,3,2,1,0:T(4,128)S(1)} %bitcast.5, f32[9,512]{1,0:T(8,128)S(1)} %get-tuple-element.16.own_ref), custom_call_target="tpu_custom_call" | custom-call | tf_op jit(solution)/shard_map/pallas_call | solution.py:282
  36.8 11.3 %all_to_all.26.gathered_ref.second_ref = f32[16,3,4,128]{3,2,1,0:T(4,128)S(1)} all-to-all(f32[16,3,4,128]{3,2,1,0:T(4,128)S(1)} %get-tuple-element.17), channel_id=1, replica_groups=mesh['tm'=32,'dom'=16] {'dom'}, dimensions={0} | all-to-all | bytes 196608 | tf_op jit(solution)/shard_map/all_to_all | solution.py:324
  48.1 3.9 %shard_map.52 = (f32[3,512]{1,0:T(4,128)S(1)}, f32[3,512]{1,0:T(4,128)S(1)}, f32[16,3,4,128]{3,2,1,0:T(4,128)S(1)}) custom-call(f32[2,8,13,4,128]{4,3,2,1,0:T(4,128)S(1)} %bitcast.6, f32[16,3,4,128]{3,2,1,0:T(4,128)S(1)} %all_to_all.26.gathered_ref.second_ref, f32[9,512]{1,0:T(8,128)S(1)} %get-tuple-element.18.velocity_ref, ...), custom_call_target="tpu_custom_call" | custom-call | tf_op jit(solution)/shard_map/pallas_call | solution.py:282
  52.1 10.9 %all_to_all.27.gathered_ref.third_ref = f32[16,3,4,128]{3,2,1,0:T(4,128)S(1)} all-to-all(f32[16,3,4,128]{3,2,1,0:T(4,128)S(1)} %get-tuple-element.20), channel_id=1, replica_groups=mesh['tm'=32,'dom'=16] {'dom'}, dimensions={0} | all-to-all | bytes 196608 | tf_op jit(solution)/shard_map/all_to_all | solution.py:333
  62.9 4.0 %shard_map.53 = f32[16,3,8,128]{3,2,1,0:T(8,128)S(1)} custom-call(f32[2,8,13,4,128]{4,3,2,1,0:T(4,128)S(1)} %bitcast.7, f32[16,3,4,128]{3,2,1,0:T(4,128)S(1)} %all_to_all.27.gathered_ref.third_ref, f32[9,512]{1,0:T(8,128)S(1)} %get-tuple-element.18.velocity_ref, f32[3,512]{1,0:T(4,128)S(1)} %get-tuple-element.21.swept_ref, ...), custom_call_target="tpu_custom_call" | custom-call | tf_op jit(solution)/shard_map/pallas_call | solution.py:282
  66.9 12.7 %all_to_all.28.quads_ref = f32[16,3,8,128]{3,2,1,0:T(8,128)S(1)} all-to-all(f32[16,3,8,128]{3,2,1,0:T(8,128)S(1)} %shard_map.53), channel_id=1, replica_groups=mesh['tm'=32,'dom'=16] {'dom'}, dimensions={0} | all-to-all | bytes 393216 | tf_op jit(solution)/shard_map/all_to_all | solution.py:343
  79.6 2.0 %shard_map.54 = (f32[15,512]{1,0:T(8,128)S(1)}, f32[32,3,4,128]{3,2,1,0:T(4,128)S(1)}) custom-call(f32[2,8,13,4,128]{4,3,2,1,0:T(4,128)S(1)} %bitcast.8, f32[16,3,4,128]{3,2,1,0:T(4,128)S(1)} %all_to_all.26.gathered_ref.second_ref, f32[16,3,4,128]{3,2,1,0:T(4,128)S(1)} %all_to_all.27.gathered_ref.third_ref, f32[16,3,8,128]{3,2,1,0:T(8,128)S(1)} %all_to_all.28.quads_ref, ...), custom_call_target="tpu_custom_call" | custom-call | tf_op jit(solution)/shard_map/pallas_call | solution.py:282
  81.7 20.5 %all_to_all.29.received_ref = f32[32,3,4,128]{3,2,1,0:T(4,128)S(1)} all-to-all(f32[32,3,4,128]{3,2,1,0:T(4,128)S(1)} %get-tuple-element.24), channel_id=1, replica_groups=mesh['tm'=32,'dom'=16] {'tm'}, dimensions={0} | all-to-all | bytes 393216 | tf_op jit(solution)/shard_map/all_to_all | solution.py:353
  102.1 0.8 shard_map.55

commit v7 on v6

--- a/solution.py
+++ b/solution.py
@@ -55,8 +55,14 @@
     return pltpu.roll(rows, rows_cycle - number, 0)
 
 
-def source_rows(p, w, leading):
-    w = w * inv_four_pi
+def strength_rows(w, leading):
+    w = cyclic(w) * inv_four_pi
+    high, low = parts_of(w, 2)
+    turned = jnp.where(leading, rotated(w, 1), rotated(w, 2))
+    return jnp.where(leading, high, low), turned
+
+
+def source_rows(p, strengths, turned, leading):
     high, low = parts_of(p, 2)
     near = jnp.where(leading, high, low)
     summed = high + low
@@ -64,11 +70,7 @@
     norms = jnp.where(leading, first, second)
     last = jnp.where(leading, third, 1.0)
     features = jnp.concatenate([near, near, norms, last], 0).astype(bf16)
-    high, low = parts_of(w, 2)
-    strengths = jnp.where(leading, high, low)
-    products = jnp.where(leading, rotated(w, 1), rotated(w, 2)) * jnp.where(
-        leading, rotated(p, 2), rotated(p, 1)
-    )
+    products = turned * jnp.where(leading, rotated(p, 2), rotated(p, 1))
     crossed = products - jnp.where(leading, rotated(products, 3), rotated(products, 5))
     high, low = parts_of(crossed, 2)
     moments = jnp.concatenate([strengths, jnp.where(leading, high, low)], 0).astype(bf16)
@@ -95,7 +97,7 @@
     total = jnp.zeros((2 * rows_cycle, width), f32)
     for begin in range(0, len(blocks), part_blocks):
         rows = [
-            source_rows(cyclic(p) - centers, cyclic(w), leading)
+            source_rows(cyclic(p) - centers, *w, leading)
             for p, w in blocks[begin : begin + part_blocks]
         ]
         features = jnp.concatenate([pair[0] for pair in rows], 1)
@@ -158,15 +160,20 @@
     spread_out(send_ref, jnp.concatenate([own, vorticity_ref[...], mine], 0))
 
 
-def nodes_kernel(all_ref, own_ref, velocity_ref, second_ref, send_ref):
+def nodes_kernel(all_ref, own_ref, velocity_ref, second_ref, send_ref, strengths_ref):
     halves, lines = all_ref.shape[:2]
+    width = own_ref.shape[1]
+    leading = lax.broadcasted_iota(jnp.int32, (rows_cycle, width), 0) < 3
+    places = [(h, z) for z in range(lines) for h in range(halves)]
+    strengths = [strength_rows(wide(all_ref, h, z, pl.ds(9, 3)), leading) for h, z in places]
+    for number, pair in enumerate(strengths):
+        strengths_ref[number] = jnp.concatenate(pair, 0)
     found = []
     for node in range(3):
         rows = pl.ds(3 * node, 3)
         blocks = [
-            (wide(all_ref, h, z, rows), wide(all_ref, h, z, pl.ds(9, 3)))
-            for z in range(lines)
-            for h in range(halves)
+            (wide(all_ref, h, z, rows), pair)
+            for (h, z), pair in zip(places, strengths, strict=True)
         ]
         found.append(field(blocks, own_ref[rows]))
     velocity_ref[...] = jnp.concatenate(found, 0)
@@ -175,20 +182,21 @@
     spread_out(send_ref, second)
 
 
-def swept_blocks(all_ref, gathered_ref):
-    halves, lines = all_ref.shape[:2]
+def swept_blocks(strengths_ref, gathered_ref):
     return [
-        (wide(gathered_ref, halves * z + h, pl.ds(0, 3)), wide(all_ref, h, z, pl.ds(9, 3)))
-        for z in range(lines)
-        for h in range(halves)
+        (
+            wide(gathered_ref, number, pl.ds(0, 3)),
+            (strengths_ref[number, 0:rows_cycle], strengths_ref[number, rows_cycle:]),
+        )
+        for number in range(gathered_ref.shape[0])
     ]
 
 
 def second_kernel(
-    all_ref, gathered_ref, velocity_ref, second_ref, swept_ref, third_ref, send_ref
+    strengths_ref, gathered_ref, velocity_ref, second_ref, swept_ref, third_ref, send_ref
 ):
     second = second_ref[...]
-    blocks = swept_blocks(all_ref, gathered_ref)
+    blocks = swept_blocks(strengths_ref, gathered_ref)
     swept = field(blocks, second)
     swept_ref[...] = swept
     nodes = [velocity_ref[pl.ds(3 * node, 3)] for node in range(3)]
@@ -198,10 +206,10 @@
 
 
 def third_kernel(
-    all_ref, gathered_ref, velocity_ref, swept_ref, third_ref, send_ref
+    strengths_ref, gathered_ref, velocity_ref, swept_ref, third_ref, send_ref
 ):
     third = third_ref[...]
-    blocks = swept_blocks(all_ref, gathered_ref)
+    blocks = swept_blocks(strengths_ref, gathered_ref)
     last = field(blocks, third)
     early = quad(node_weights[0], velocity_ref[0:3], swept_ref[...], last)
     late = quad(node_weights[1], velocity_ref[0:3], swept_ref[...], last)
@@ -318,14 +326,14 @@
     everyone = lax.all_gather(along, "dom", axis=0, axis_index_groups=same_chip)
     three = (3, width)
     packed = (3, chunks, lane)
-    velocity, second, send = call(
-        nodes_kernel, [(9, width), three, (domains,) + packed], everyone, own
+    velocity, second, send, strengths = call(
+        nodes_kernel, [(9, width), three, (domains,) + packed, (domains, 2 * rows_cycle, width)], everyone, own
     )
     seconds = lax.all_to_all(send, "dom", 0, 0)
     swept, third, send = call(
         second_kernel,
         [three, three, (domains,) + packed],
-        everyone,
+        strengths,
         seconds,
         velocity,
         second,
@@ -334,7 +342,7 @@
     (send,) = call(
         third_kernel,
         [(domains, 3, 2 * chunks, lane)],
-        everyone,
+        strengths,
         thirds,
         velocity,
         swept,

time: 103 us -> 103 us (level)
  no operation moved by 1% of the time
where the time goes in v7:
time: 103 us
  blocking collectives  79.5 us (77%)
  Pallas kernels  22.8 us (22%)
    pallas_call x5, Pallas kernels, call(): pl.pallas_call(kernel, out_shape=[jax.ShapeDtypeStruct(shape, f32) for sh...  21.9 us
    all_to_all x1, blocking collectives, body(): received = lax.all_to_all(send, 'tm', 0, 0)  20.5 us
    all_to_all x1, blocking collectives, body(): along = lax.all_to_all(send, 'dom', 0, 0, axis_index_groups=same_core)  19.7 us
    all_to_all x1, blocking collectives, body(): quads = lax.all_to_all(send, 'dom', 0, 0)  12.7 us
    all_to_all x1, blocking collectives, body(): seconds = lax.all_to_all(send, 'dom', 0, 0)  11.3 us
    all_to_all x1, blocking collectives, body(): thirds = lax.all_to_all(send, 'dom', 0, 0)  10.9 us
    all_gather x1, blocking collectives, body(): everyone = lax.all_gather(along, 'dom', axis=0, axis_index_groups=same_chip)  4.48 us

profile of v7, /device:TPU:1, one launch (start us, length us, event | category | flops | bytes accessed | tf_op | source)
XLA Modules:
  0.0 103.0 jit_solution(8769041580842298122)
XLA Ops:
  0.6 0.9 shard_map.50
  1.5 19.7 %all_to_all.25 = f32[8,13,4,128]{3,2,1,0:T(4,128)S(1)} all-to-all(f32[8,13,4,128]{3,2,1,0:T(4,128)S(1)} %get-tuple-element.16), channel_id=1, replica_groups={{0,2,4,6,8,10,12,14},{1,3,5,7,9,11,13,15},{16,18,20,22,24,26,28,30},{17..., dimensions={0} | all-to-all | bytes 425984 | tf_op jit(solution)/shard_map/all_to_all | solution.py:325
  21.2 4.5 %all-gather = f32[16,13,4,128]{3,2,1,0:T(4,128)S(1)} all-gather(f32[8,13,4,128]{3,2,1,0:T(4,128)S(1)} %all_to_all.25), channel_id=2, replica_groups={{0,1},{2,3},{4,5},{6,7},{8,9},{10,11},{12,13},{14,15},{16,17},{18,19},{..., dimensions={0}, use_global_device_ids=true | all-gather | bytes 638976 | tf_op jit(solution)/shard_map/all_gather | solution.py:326
  25.7 11.1 %shard_map.51 = (f32[9,512]{1,0:T(8,128)S(1)}, f32[3,512]{1,0:T(4,128)S(1)}, f32[16,3,4,128]{3,2,1,0:T(4,128)S(1)}, f32[16,16,512]{2,1,0:T(8,128)S(1)}) custom-call(f32[2,8,13,4,128]{4,3,2,1,0:T(4,128)S(1)} %bitcast.5, f32[9,512]{1,0:T(8,128)S(1)} %get-tuple-element.17.own_ref), custom_call_target="tpu_custom_call" | custom-call | tf_op jit(solution)/shard_map/pallas_call | solution.py:290
  36.8 11.3 %all_to_all.26.gathered_ref.second_ref = f32[16,3,4,128]{3,2,1,0:T(4,128)S(1)} all-to-all(f32[16,3,4,128]{3,2,1,0:T(4,128)S(1)} %get-tuple-element.18), channel_id=1, replica_groups=mesh['tm'=32,'dom'=16] {'dom'}, dimensions={0} | all-to-all | bytes 196608 | tf_op jit(solution)/shard_map/all_to_all | solution.py:332
  48.1 3.9 %shard_map.52 = (f32[3,512]{1,0:T(4,128)S(1)}, f32[3,512]{1,0:T(4,128)S(1)}, f32[16,3,4,128]{3,2,1,0:T(4,128)S(1)}) custom-call(f32[16,16,512]{2,1,0:T(8,128)S(1)} %get-tuple-element.19.strengths_ref, f32[16,3,4,128]{3,2,1,0:T(4,128)S(1)} %all_to_all.26.gathered_ref.second_ref, f32[9,512]{1,0:T(8,128)S(1)} %get-tuple-element.20.velocity_ref, ...), custom_call_target="tpu_custom_call" | custom-call | tf_op jit(solution)/shard_map/pallas_call | solution.py:290
  52.1 10.9 %all_to_all.27.gathered_ref.third_ref = f32[16,3,4,128]{3,2,1,0:T(4,128)S(1)} all-to-all(f32[16,3,4,128]{3,2,1,0:T(4,128)S(1)} %get-tuple-element.22), channel_id=1, replica_groups=mesh['tm'=32,'dom'=16] {'dom'}, dimensions={0} | all-to-all | bytes 196608 | tf_op jit(solution)/shard_map/all_to_all | solution.py:341
  62.9 4.0 %shard_map.53 = f32[16,3,8,128]{3,2,1,0:T(8,128)S(1)} custom-call(f32[16,16,512]{2,1,0:T(8,128)S(1)} %get-tuple-element.19.strengths_ref, f32[16,3,4,128]{3,2,1,0:T(4,128)S(1)} %all_to_all.27.gathered_ref.third_ref, f32[9,512]{1,0:T(8,128)S(1)} %get-tuple-element.20.velocity_ref, f32[3,512]{1,0:T(4,128)S(1)} %get-tuple-element.23.swept_ref, ...), custom_call_target="tpu_custom_call" | custom-call | tf_op jit(solution)/shard_map/pallas_call | solution.py:290
  66.9 12.7 %all_to_all.28.quads_ref = f32[16,3,8,128]{3,2,1,0:T(8,128)S(1)} all-to-all(f32[16,3,8,128]{3,2,1,0:T(8,128)S(1)} %shard_map.53), channel_id=1, replica_groups=mesh['tm'=32,'dom'=16] {'dom'}, dimensions={0} | all-to-all | bytes 393216 | tf_op jit(solution)/shard_map/all_to_all | solution.py:351
  79.6 2.0 %shard_map.54 = (f32[15,512]{1,0:T(8,128)S(1)}, f32[32,3,4,128]{3,2,1,0:T(4,128)S(1)}) custom-call(f32[2,8,13,4,128]{4,3,2,1,0:T(4,128)S(1)} %bitcast.6, f32[16,3,4,128]{3,2,1,0:T(4,128)S(1)} %all_to_all.26.gathered_ref.second_ref, f32[16,3,4,128]{3,2,1,0:T(4,128)S(1)} %all_to_all.27.gathered_ref.third_ref, f32[16,3,8,128]{3,2,1,0:T(8,128)S(1)} %all_to_all.28.quads_ref, ...), custom_call_target="tpu_custom_call" | custom-call | tf_op jit(solution)/shard_map/pallas_call | solution.py:290
  81.7 20.5 %all_to_all.29.received_ref = f32[32,3,4,128]{3,2,1,0:T(4,128)S(1)} all-to-all(f32[32,3,4,128]{3,2,1,0:T(4,128)S(1)} %get-tuple-element.26), channel_id=1, replica_groups=mesh['tm'=32,'dom'=16] {'tm'}, dimensions={0} | all-to-all | bytes 393216 | tf_op jit(solution)/shard_map/all_to_all | solution.py:361
  102.2 0.8 shard_map.55
